TPU v7x, 32 devices: a whole 2x2x4 slice. The times are simulated.
32 devices in a mesh: seq: 16 (over z, x, core), blk: 2 (over y).
Axes of the slice: x: 2, y: 2, z: 4, core: 2. Of those that a mesh axis runs over, the one named last changes fastest.
Arguments:
- tokens: bfloat16 [16, 1024, 768], P('seq', 'blk'), may hold values from -6 to 6
- lengths: int32 [16, 4], P('seq'), may hold values from 32 to 768, as said below
- padding: int32 [16, 1024], P('seq', 'blk'), may hold values 0 or 1
- cotangent: bfloat16 [16, 1024, 768], P('seq', 'blk'), may hold values from -6 to 6
- ln1_gain: float32 [768], replicated, may hold values from 0.5 to 1.5
- ln1_bias: float32 [768], replicated, may hold values from -1 to 1
- w_qkv: bfloat16 [768, 2304], replicated, may hold values from -0.21875 to 0.21875
- q_bias: float32 [768], replicated, may hold values from -3 to 3
- v_bias: float32 [768], replicated, may hold values from -3 to 3
- w_out: bfloat16 [768, 768], replicated, may hold values from -6 to 6
- out_bias: float32 [768], replicated, may hold values from -2 to 2
- ln2_gain: float32 [768], replicated, may hold values from 0.5 to 1.5
- ln2_bias: float32 [768], replicated, may hold values from -1 to 1
- w_fc1: bfloat16 [768, 3072], replicated, may hold values from -0.21875 to 0.21875
- fc1_bias: float32 [3072], replicated, may hold values from -3 to 3
- w_fc2: bfloat16 [3072, 768], replicated, may hold values from -0.109375 to 0.109375
- fc2_bias: float32 [768], replicated, may hold values from -2 to 2
Outputs:
- result: bfloat16 [16, 1024, 768], P('seq', 'blk')
- grad_tokens: bfloat16 [16, 1024, 768], P('seq', 'blk')
- grad_ln1_gain: float32 [768], P(('seq', 'blk'))
- grad_ln1_bias: float32 [768], P(('seq', 'blk'))
- grad_w_qkv: float32 [768, 2304], P(('seq', 'blk'))
- grad_q_bias: float32 [768], P(('seq', 'blk'))
- grad_v_bias: float32 [768], P(('seq', 'blk'))
- grad_w_out: float32 [768, 768], P(('seq', 'blk'))
- grad_out_bias: float32 [768], P(('seq', 'blk'))
- grad_ln2_gain: float32 [768], P(('seq', 'blk'))
- grad_ln2_bias: float32 [768], P(('seq', 'blk'))
- grad_w_fc1: float32 [768, 3072], P(('seq', 'blk'))
- grad_fc1_bias: float32 [3072], P(('seq', 'blk'))
- grad_w_fc2: float32 [3072, 768], P(('seq', 'blk'))
- grad_fc2_bias: float32 [768], P(('seq', 'blk'))
Inputs may be any that keep to these rules, and one draw needn't show every extreme that they name: In each packed sequence the 4 clip lengths sum to 1024; one clip, a long video whose visible patches fill 1024 - 512 // 2 tokens, stands at a place drawn from the seed, and three short clips share the remaining 512 // 2.
All inputs are finite; a program needn't handle non-finite values. No bound on the sum of `padding` on one device may be relied on, other than what follows from the above.
Results may differ from a plain program's by a relative error of at most 0.014.
Values may be sent and summed in bfloat16 or wider, within the bound.
A program may use at most 256 MiB of HBM per device.

v0:
```python
import functools

import jax
import jax.numpy as jnp
from jax import lax
from jax.experimental import pallas as pl
from jax.experimental.pallas import tpu as pltpu
from jax.sharding import PartitionSpec as P

D = 768
FF = 3072
HEADS = 12
HEAD_DIM = 64


epsilon = 1e-06
score_scale = 0.125
masked_score = -1e30


def clip_numbers(clip_lengths, positions):
    bounds = jnp.cumsum(clip_lengths)
    return jnp.sum((positions[:, None] >= bounds[None, :]).astype(jnp.int32), axis=1)


def normalize(values, scales, offset):
    center = values - jnp.mean(values, axis=-1, keepdims=True)
    spread = jnp.mean(center * center, axis=-1, keepdims=True)
    inverse = lax.rsqrt(spread + epsilon)
    unit = center * inverse
    return (unit * scales + offset, unit, inverse)


def norm_back(upstream, unit, inverse, scales):
    scaled = upstream * scales
    return inverse * (
        scaled
        - jnp.mean(scaled, axis=-1, keepdims=True)
        - unit * jnp.mean(scaled * unit, axis=-1, keepdims=True)
    )


def gelu_slope(pre_gelu):
    cdf_part = 0.5 * (1.0 + lax.erf(pre_gelu * 0.7071067811865476))
    return cdf_part + pre_gelu * jnp.exp(-0.5 * pre_gelu * pre_gelu) * 0.3989422804014327


def masked_scores(query_heads, key_heads, clip_ids, positions, block_tags, key_pos):
    raw_scores = (
        jnp.einsum("qhd,khd->qhk", query_heads, key_heads, preferred_element_type=jnp.float32)
        * score_scale
    )
    allowed = (block_tags[None, :] == clip_ids[:, None]) | (positions[:, None] == key_pos[None, :])
    return jnp.where(allowed[:, None, :], raw_scores, masked_score)


def score_grads(
    query_heads,
    key_heads,
    value_heads,
    grad_heads,
    log_total,
    row_delta,
    clip_ids,
    positions,
    block_tags,
    key_pos,
):
    scores = masked_scores(query_heads, key_heads, clip_ids, positions, block_tags, key_pos)
    attn_probs = jnp.exp(scores - log_total[..., None])
    grad_probs = jnp.einsum(
        "qhd,khd->qhk", grad_heads, value_heads, preferred_element_type=jnp.float32
    )
    grad_scores = (attn_probs * (grad_probs - row_delta[..., None])).astype(jnp.bfloat16)
    return (attn_probs, grad_scores)


def stage_orders():
    seq_bits = lax.axis_size("seq").bit_length() - 1
    blk_bits = lax.axis_size("blk").bit_length() - 1
    seq_stages = [blk_bits + b for b in range(seq_bits)]
    blk_stages = list(range(blk_bits))
    one = seq_stages[:2] + blk_stages + seq_stages[2:]
    two = seq_stages[:1] + blk_stages + seq_stages[1:]
    return one, two


def scatter_stages(terms, order):
    n_dev = terms.shape[0]
    bits = n_dev.bit_length() - 1
    me = lax.axis_index("seq") * lax.axis_size("blk") + lax.axis_index("blk")
    rest = terms.shape[1:]
    kind = terms.dtype
    held = terms.reshape((2,) * bits + rest)
    for number, bit in enumerate(order):
        axis = bits - 1 - bit
        mine = (me >> bit) & 1
        sent = lax.dynamic_slice_in_dim(held, 1 - mine, 1, axis)
        kept = lax.dynamic_slice_in_dim(held, mine, 1, axis)
        swap = [(i, i ^ (1 << bit)) for i in range(n_dev)]
        came = lax.ppermute(sent, ("seq", "blk"), swap)
        total = kept.astype(jnp.float32) + came.astype(jnp.float32)
        held = total if number == bits - 1 else total.astype(kind)
    return held.reshape((1,) + rest)


def scatter_sum(grad):
    n_dev = lax.axis_size("seq") * lax.axis_size("blk")
    rows, width = grad.shape
    terms = grad.astype(jnp.bfloat16).reshape(n_dev, rows // n_dev, width)
    one, two = stage_orders()
    left = scatter_stages(terms[:, :, : width // 2], one)[0]
    right = scatter_stages(terms[:, :, width // 2 :], two)[0]
    return jnp.concatenate([left, right], axis=1)


def body(
    tokens,
    lengths,
    padding,
    cotangent,
    ln1_gain,
    ln1_bias,
    w_qkv,
    q_bias,
    v_bias,
    w_out,
    out_bias,
    ln2_gain,
    ln2_bias,
    w_fc1,
    fc1_bias,
    w_fc2,
    fc2_bias,
):
    tok_rows = tokens.shape[1]
    group_size = lax.axis_size("blk")
    n_dev = lax.axis_size("seq") * group_size
    positions = lax.axis_index("blk") * tok_rows + jnp.arange(tok_rows, dtype=jnp.int32)
    clip_ids = clip_numbers(lengths[0], positions)
    key_tags = jnp.where(padding[0] == 1, -1, clip_ids)
    tokens_f32 = tokens[0].astype(jnp.float32)
    first_norm, unit_one, inverse_one = normalize(tokens_f32, ln1_gain, ln1_bias)
    normed_one = first_norm.astype(jnp.bfloat16)
    joint_bias = jnp.concatenate([q_bias, jnp.zeros_like(q_bias), v_bias])
    projected = (
        jnp.dot(normed_one, w_qkv, preferred_element_type=jnp.float32) + joint_bias
    ).astype(jnp.bfloat16)
    keys_own = projected[:, D : 2 * D]
    values_own = projected[:, 2 * D :]
    query_heads = projected[:, :D].reshape(tok_rows, HEADS, HEAD_DIM)
    starts = jnp.arange(group_size, dtype=jnp.int32) * tok_rows

    def fold_keys(running, key_block, offset):
        block_keys, block_values, block_tags = key_block
        key_count = block_keys.shape[0]
        key_pos = offset + jnp.arange(key_count, dtype=jnp.int32)
        scores = masked_scores(
            query_heads,
            block_keys.reshape(key_count, HEADS, HEAD_DIM),
            clip_ids,
            positions,
            block_tags,
            key_pos,
        )
        row_max, row_sum, weighted = running
        new_max = jnp.maximum(row_max, jnp.max(scores, axis=-1))
        rescale = jnp.exp(row_max - new_max)
        exp_scores = jnp.exp(scores - new_max[..., None])
        row_sum = row_sum * rescale + jnp.sum(exp_scores, axis=-1)
        weighted = weighted * rescale[..., None] + jnp.einsum(
            "qhk,khd->qhd",
            exp_scores.astype(jnp.bfloat16),
            block_values.reshape(key_count, HEADS, HEAD_DIM),
            preferred_element_type=jnp.float32,
        )
        return (new_max, row_sum, weighted)

    start_state = (
        jnp.full((tok_rows, HEADS), masked_score, jnp.float32),
        jnp.zeros((tok_rows, HEADS), jnp.float32),
        jnp.zeros((tok_rows, HEADS, HEAD_DIM), jnp.float32),
    )
    group_keys, group_values, group_tags = (
        lax.all_gather(keys_own, "blk", axis=0, tiled=True),
        lax.all_gather(values_own, "blk", axis=0, tiled=True),
        lax.all_gather(key_tags, "blk", axis=0, tiled=True),
    )

    def scan_fold(running, scan_args):
        return (fold_keys(running, (scan_args[0], scan_args[1], scan_args[2]), scan_args[3]), None)

    final_state = lax.scan(
        scan_fold,
        start_state,
        (
            group_keys.reshape(group_size, tok_rows, D),
            group_values.reshape(group_size, tok_rows, D),
            group_tags.reshape(group_size, tok_rows),
            starts,
        ),
    )[0]
    row_max, row_sum, weighted = final_state
    mixed_f32 = weighted / row_sum[..., None]
    log_total = row_max + jnp.log(row_sum)
    mixed = mixed_f32.reshape(tok_rows, D).astype(jnp.bfloat16)
    residual = tokens_f32 + jnp.dot(mixed, w_out, preferred_element_type=jnp.float32) + out_bias
    second_norm, unit_two, inverse_two = normalize(residual, ln2_gain, ln2_bias)
    normed_two = second_norm.astype(jnp.bfloat16)
    pre_gelu = jnp.dot(normed_two, w_fc1, preferred_element_type=jnp.float32) + fc1_bias
    activated = jax.nn.gelu(pre_gelu, approximate=False).astype(jnp.bfloat16)
    result = (
        residual + jnp.dot(activated, w_fc2, preferred_element_type=jnp.float32) + fc2_bias
    ).astype(jnp.bfloat16)
    grad_out = cotangent[0]
    grad_fc2_bias = jnp.sum(grad_out, axis=0, dtype=jnp.float32)
    grad_w_fc2 = jnp.einsum("tf,td->fd", activated, grad_out, preferred_element_type=jnp.float32)
    grad_act = jnp.einsum("td,fd->tf", grad_out, w_fc2, preferred_element_type=jnp.float32)
    grad_pre = (grad_act * gelu_slope(pre_gelu)).astype(jnp.bfloat16)
    grad_fc1_bias = jnp.sum(grad_pre, axis=0, dtype=jnp.float32)
    grad_w_fc1 = jnp.einsum("td,tf->df", normed_two, grad_pre, preferred_element_type=jnp.float32)
    grad_norm_two = jnp.einsum("tf,df->td", grad_pre, w_fc1, preferred_element_type=jnp.float32)
    grad_ln2_gain = jnp.sum(grad_norm_two * unit_two, axis=0)
    grad_ln2_bias = jnp.sum(grad_norm_two, axis=0)
    grad_residual = grad_out.astype(jnp.float32) + norm_back(
        grad_norm_two, unit_two, inverse_two, ln2_gain
    )
    grad_branch = grad_residual.astype(jnp.bfloat16)
    grad_out_bias = jnp.sum(grad_branch, axis=0, dtype=jnp.float32)
    grad_w_out = jnp.einsum("td,te->de", mixed, grad_branch, preferred_element_type=jnp.float32)
    grad_mixed = jnp.einsum(
        "te,de->td", grad_branch, w_out, preferred_element_type=jnp.float32
    ).astype(jnp.bfloat16)
    grad_heads = grad_mixed.reshape(tok_rows, HEADS, HEAD_DIM)
    row_delta = jnp.sum(grad_heads * mixed_f32, axis=-1)
    key_stack = (
        group_keys.reshape(group_size, tok_rows, D),
        group_values.reshape(group_size, tok_rows, D),
        group_tags.reshape(group_size, tok_rows),
        starts,
    )

    def back_block(grad_queries, scan_args):
        block_keys, block_values, block_tags, offset = scan_args
        key_pos = offset + jnp.arange(tok_rows, dtype=jnp.int32)
        key_heads = block_keys.reshape(tok_rows, HEADS, HEAD_DIM)
        value_heads = block_values.reshape(tok_rows, HEADS, HEAD_DIM)
        attn_probs, grad_scores = score_grads(
            query_heads,
            key_heads,
            value_heads,
            grad_heads,
            log_total,
            row_delta,
            clip_ids,
            positions,
            block_tags,
            key_pos,
        )
        grad_values = jnp.einsum(
            "qhk,qhd->khd",
            attn_probs.astype(jnp.bfloat16),
            grad_heads,
            preferred_element_type=jnp.float32,
        )
        grad_queries = (
            grad_queries
            + jnp.einsum("qhk,khd->qhd", grad_scores, key_heads, preferred_element_type=jnp.float32)
            * score_scale
        )
        grad_keys = (
            jnp.einsum("qhk,qhd->khd", grad_scores, query_heads, preferred_element_type=jnp.float32)
            * score_scale
        )
        return (
            grad_queries,
            jnp.concatenate(
                [grad_keys.reshape(tok_rows, D), grad_values.reshape(tok_rows, D)], axis=1
            ),
        )

    grad_queries, key_terms = lax.scan(
        back_block, jnp.zeros((tok_rows, HEADS, HEAD_DIM), jnp.float32), key_stack
    )
    key_sums = lax.psum_scatter(
        key_terms.reshape(group_size * tok_rows, 2 * D).astype(jnp.bfloat16),
        "blk",
        scatter_dimension=0,
        tiled=True,
    )
    grad_qkv = jnp.concatenate(
        [grad_queries.reshape(tok_rows, D).astype(jnp.bfloat16), key_sums], axis=1
    )
    grad_q_bias = jnp.sum(grad_qkv[:, :D], axis=0, dtype=jnp.float32)
    grad_v_bias = jnp.sum(grad_qkv[:, 2 * D :], axis=0, dtype=jnp.float32)
    grad_w_qkv = jnp.einsum("td,te->de", normed_one, grad_qkv, preferred_element_type=jnp.float32)
    grad_norm_one = jnp.einsum("te,de->td", grad_qkv, w_qkv, preferred_element_type=jnp.float32)
    grad_ln1_gain = jnp.sum(grad_norm_one * unit_one, axis=0)
    grad_ln1_bias = jnp.sum(grad_norm_one, axis=0)
    grad_tokens = (
        grad_residual + norm_back(grad_norm_one, unit_one, inverse_one, ln1_gain)
    ).astype(jnp.bfloat16)
    small = jnp.concatenate(
        [
            v.reshape(n_dev, -1)
            for v in (
                grad_ln1_gain,
                grad_ln1_bias,
                grad_q_bias,
                grad_v_bias,
                grad_out_bias,
                grad_ln2_gain,
                grad_ln2_bias,
                grad_fc1_bias,
                grad_fc2_bias,
            )
        ],
        axis=1,
    )
    sum_fc2 = scatter_sum(grad_w_fc2)
    sum_fc1 = scatter_sum(grad_w_fc1)
    sum_out = scatter_sum(grad_w_out)
    sum_qkv = scatter_sum(grad_w_qkv)
    part = D // n_dev
    small = scatter_stages(small, stage_orders()[0])[0]
    pieces = []
    at = 0
    for size in (part, part, part, part, part, part, part, FF // n_dev, part):
        pieces.append(small[at : at + size])
        at += size
    summed = (
        pieces[0],
        pieces[1],
        sum_qkv,
        pieces[2],
        pieces[3],
        sum_out,
        pieces[4],
        pieces[5],
        pieces[6],
        sum_fc1,
        pieces[7],
        sum_fc2,
        pieces[8],
    )
    return (
        result[None],
        grad_tokens[None],
        summed[0],
        summed[1],
        summed[2],
        summed[3],
        summed[4],
        summed[5],
        summed[6],
        summed[7],
        summed[8],
        summed[9],
        summed[10],
        summed[11],
        summed[12],
    )


f32 = jnp.float32
bf16 = jnp.bfloat16
MESH = pl.DeviceIdType.MESH
PAIRS = HEADS // 2
RING = 4
FF_CHUNK = 512
ROW_TILE = 128


def fits(mesh):
    return dict(mesh.shape) == {"seq": 16, "blk": 2}


def dot(a, b):
    return lax.dot_general(a, b, (((1,), (0,)), ((), ())), preferred_element_type=f32)


def dot_nt(a, b):
    return lax.dot_general(a, b, (((1,), (1,)), ((), ())), preferred_element_type=f32)


def dot_tn(a, b):
    return lax.dot_general(a, b, (((0,), (0,)), ((), ())), preferred_element_type=f32)


def unit_of(values):
    center = values - jnp.mean(values, axis=1, keepdims=True)
    inverse = lax.rsqrt(jnp.mean(center * center, axis=1, keepdims=True) + epsilon)
    return center * inverse, inverse


def row(ref):
    return ref[...].reshape(1, ref.shape[0])


def column_sum(values):
    return jnp.sum(values, axis=0, keepdims=True)


def block_kernel(
    tok_hbm,
    len_ref,
    pad_ref,
    cot_hbm,
    ln1_gain,
    ln1_bias,
    wqkv_hbm,
    q_bias,
    v_bias,
    wout_hbm,
    out_bias,
    ln2_gain,
    ln2_bias,
    wfc1_hbm,
    fc1_bias,
    wfc2_hbm,
    fc2_bias,
    result_ref,
    gtok_ref,
    vec_ref,
    fb1_ref,
    gfc1_hbm,
    gfc2_hbm,
    gqo_hbm,
    e_hbm,
    wqkv,
    wout,
    wfc1,
    wfc2,
    tok,
    tokp,
    cot,
    nrm,
    nrm_t,
    nrm2_t,
    qkv,
    kvp,
    gm,
    bias,
    ering,
    slots,
    gfc1,
    gfc2,
    gn_out,
    gn_in,
    tags,
    load_sem,
    e_sem,
    out_sem,
    send_sem,
    recv_sem,
):
    rows = tok.shape[0]
    seq = lax.axis_index("seq")
    blk = lax.axis_index("blk")
    twin = (seq, 1 - blk)

    loads = [
        pltpu.make_async_copy(src, dst, load_sem.at[i])
        for i, (src, dst) in enumerate(
            (
                (tok_hbm.at[0], tok),
                (wqkv_hbm, wqkv),
                (wout_hbm, wout),
                (wfc1_hbm, wfc1),
                (wfc2_hbm, wfc2),
                (cot_hbm.at[0], cot),
            )
        )
    ]
    for copy in loads:
        copy.start()

    ends = []
    total = jnp.int32(0)
    for i in range(len_ref.shape[1]):
        total = total + len_ref[0, i]
        ends.append(total)

    def clips_at(positions):
        number = jnp.zeros_like(positions)
        for end in ends:
            number = number + jnp.where(positions >= end, 1, 0)
        return number

    base = blk * rows
    lane_pos = base + lax.broadcasted_iota(jnp.int32, (8, rows), 1)
    padding = jnp.broadcast_to(pad_ref[...], (8, rows))
    tags[0] = jnp.where(padding == 1, -1, clips_at(lane_pos))

    barrier = pltpu.get_barrier_semaphore()
    pl.semaphore_signal(barrier, inc=1, device_id=twin, device_id_type=MESH)
    pl.semaphore_wait(barrier, 1)

    def to_twin(i, src, dst):
        return pltpu.make_async_remote_copy(
            src_ref=src,
            dst_ref=dst,
            send_sem=send_sem.at[i],
            recv_sem=recv_sem.at[i],
            device_id=twin,
            device_id_type=MESH,
        )

    send_tok = to_twin(0, tok_hbm.at[0], tokp)
    send_tags = to_twin(1, tags.at[0], tags.at[1])
    send_tags.start()
    send_tok.start()

    row_tiles = rows // ROW_TILE

    def tile(t):
        return pl.ds(pl.multiple_of(t * ROW_TILE, ROW_TILE), ROW_TILE)

    def first_norm(src, part):
        gain, offset = row(ln1_gain), row(ln1_bias)

        def step(t, carry):
            unit, _ = unit_of(src[tile(t), :].astype(f32))
            normed = (unit * gain + offset).astype(bf16)
            nrm[tile(t), :] = normed
            at = pl.multiple_of(part * rows + t * ROW_TILE, ROW_TILE)
            nrm_t[:, pl.ds(at, ROW_TILE)] = normed.T
            return carry

        lax.fori_loop(0, row_tiles, step, 0)

    def set_bias(part):
        clip_col = clips_at(base + lax.broadcasted_iota(jnp.int32, (rows, rows), 0))
        tag_row = jnp.broadcast_to(tags[part, 0:1, :], (rows, rows))
        allowed = tag_row == clip_col
        if part == 0:
            here = lax.broadcasted_iota(jnp.int32, (rows, rows), 0)
            there = lax.broadcasted_iota(jnp.int32, (rows, rows), 1)
            allowed = allowed | (here == there)
        bias[...] = jnp.where(allowed, 0.0, masked_score)

    loads[0].wait()
    first_norm(tok, 0)
    set_bias(0)
    loads[1].wait()
    wide = 256

    def project(kind, add, scale, dst, dst_at):
        def step(c, carry):
            col = pl.multiple_of(c * wide, wide)
            out = dot(nrm[...], wqkv[:, pl.ds(kind * D + col, wide)])
            if add is not None:
                out = out + add[pl.ds(col, wide)].reshape(1, wide)
            out = out.astype(bf16)
            if scale:
                out = out * jnp.bfloat16(score_scale)
            dst[:, pl.ds(dst_at + col, wide)] = out
            return carry

        lax.fori_loop(0, D // wide, step, 0)

    project(0, q_bias, True, qkv, 0)
    project(1, None, False, qkv, D)
    project(2, v_bias, False, qkv, 2 * D)

    low_lane = lax.broadcasted_iota(jnp.int32, (rows, 128), 1) < 64

    def half(values, h):
        return jnp.where(low_lane if h == 0 else ~low_lane, values, jnp.zeros_like(values))

    def e_copy(number, slot, out):
        if out:
            return pltpu.make_async_copy(ering.at[slot], e_hbm.at[number], e_sem.at[slot])
        return pltpu.make_async_copy(e_hbm.at[number], ering.at[slot], e_sem.at[slot])

    MIXED, F_OWN, F_TWIN, RES, ACC, GNT = range(6)

    def forward_pair(part, hp, key_ref, key_at, value_at):
        col = pl.multiple_of(hp * 128, 128)
        cols = pl.ds(col, 128)
        number = part * PAIRS + hp
        slot = number % RING

        @pl.when(number >= RING)
        def _():
            e_copy(number - RING, slot, True).wait()

        q = qkv[:, cols]
        k = key_ref[:, pl.ds(key_at + col, 128)]
        v = key_ref[:, pl.ds(value_at + col, 128)]
        outs, tops = [], []
        for h in range(2):
            scores = dot_nt(q, half(k, h)) + bias[...]
            top = jnp.max(scores, axis=1, keepdims=True)
            e = jnp.exp(scores - top).astype(bf16)
            ering[slot, h] = e
            ones = jnp.ones_like(v)
            outs.append(dot(e, jnp.where(low_lane if h == 0 else ~low_lane, v, ones)))
            tops.append(top)
        e_copy(number, slot, True).start()
        weighted = jnp.where(low_lane, outs[0], outs[1])
        sums = pltpu.roll(jnp.where(low_lane, outs[1], outs[0]), 64, 1)
        top = jnp.where(low_lane, tops[0], tops[1])
        if part == 0:
            slots[MIXED, :, cols] = weighted
            slots[F_OWN, :, cols] = sums
            slots[F_TWIN, :, cols] = top
        else:
            top_own = slots[F_TWIN, :, cols]
            both = jnp.maximum(top_own, top)
            scale_own = jnp.exp(top_own - both)
            scale_twin = jnp.exp(top - both)
            inverse = 1.0 / (scale_own * slots[F_OWN, :, cols] + scale_twin * sums)
            scale_own = scale_own * inverse
            scale_twin = scale_twin * inverse
            slots[MIXED, :, cols] = scale_own * slots[MIXED, :, cols] + scale_twin * weighted
            slots[F_OWN, :, cols] = scale_own
            slots[F_TWIN, :, cols] = scale_twin

    def pairs_loop(body):
        def step(hp, carry):
            body(hp)
            return carry

        lax.fori_loop(0, PAIRS, step, 0)

    pairs_loop(lambda hp: forward_pair(0, hp, qkv, D, 2 * D))

    send_tok.wait()
    send_tags.wait()
    first_norm(tokp, 1)
    set_bias(1)
    project(1, None, False, kvp, 0)
    project(2, v_bias, False, kvp, D)
    pairs_loop(lambda hp: forward_pair(1, hp, kvp, 0, D))

    loads[2].wait()

    def branch(c, carry):
        cols = pl.ds(pl.multiple_of(c * wide, wide), wide)
        out = dot(slots[MIXED].astype(bf16), wout[:, cols])
        out = out + out_bias[cols].reshape(1, wide)
        slots[RES, :, cols] = tok[:, cols].astype(f32) + out
        return carry

    lax.fori_loop(0, D // wide, branch, 0)
    gain_two, offset_two = row(ln2_gain), row(ln2_bias)

    def second_norm(t, carry):
        unit, _ = unit_of(slots[RES, tile(t), :])
        normed = (unit * gain_two + offset_two).astype(bf16)
        nrm[tile(t), :] = normed
        nrm2_t[:, tile(t)] = normed.T
        slots[ACC, tile(t), :] = jnp.zeros((ROW_TILE, D), f32)
        slots[GNT, tile(t), :] = jnp.zeros((ROW_TILE, D), f32)
        return carry

    lax.fori_loop(0, row_tiles, second_norm, 0)

    loads[3].wait()
    loads[4].wait()
    loads[5].wait()

    def feed(c, carry):
        units = pl.ds(pl.multiple_of(c * FF_CHUNK, FF_CHUNK), FF_CHUNK)
        w1 = wfc1[:, units]
        w2 = wfc2[units, :]
        pre = dot(nrm[...], w1) + fc1_bias[units].reshape(1, FF_CHUNK)
        phi = 0.5 * (1.0 + lax.erf(pre * 0.7071067811865476))
        slope = phi + pre * jnp.exp(-0.5 * pre * pre) * 0.3989422804014327
        activated = (pre * phi).astype(bf16)
        grad_pre = (dot_nt(cot[...], w2) * slope).astype(bf16)
        slots[ACC] += dot(activated, w2)
        slots[GNT] += dot_nt(grad_pre, w1)
        gfc2[units, :] = dot_tn(activated, cot[...]).astype(bf16)
        gfc1[:, units] = dot(nrm2_t[...], grad_pre).astype(bf16)
        fb1_ref[:, units] = column_sum(grad_pre.astype(f32))
        return carry

    lax.fori_loop(0, FF // FF_CHUNK, feed, 0)
    store_fc1 = pltpu.make_async_copy(gfc1, gfc1_hbm, out_sem.at[0])
    store_fc2 = pltpu.make_async_copy(gfc2, gfc2_hbm, out_sem.at[1])
    store_fc1.start()
    store_fc2.start()

    for number in range(2 * PAIRS - RING, 2 * PAIRS):
        e_copy(number, number % RING, True).wait()
    back_order = [PAIRS + hp for hp in range(PAIRS)] + list(range(PAIRS))

    def e_number(step):
        return lax.rem(step + PAIRS, 2 * PAIRS)

    for step in range(RING):
        e_copy(back_order[step], step % RING, False).start()

    vec_ref[...] = jnp.zeros(vec_ref.shape, f32)
    (V_LN1G, V_LN1B, V_QB, V_VB, V_OB, V_LN2G, V_LN2B, V_FC2B) = range(8)

    def add_vec(kind, values):
        vec_ref[kind : kind + 1, :] += column_sum(values)

    def second_back(t, carry):
        here = tile(t)
        unit, inverse = unit_of(slots[RES, here, :])
        result_ref[0, here, :] = (
            slots[RES, here, :] + slots[ACC, here, :] + row(fc2_bias)
        ).astype(bf16)
        upstream = slots[GNT, here, :]
        grad_out = cot[here, :].astype(f32)
        add_vec(V_FC2B, grad_out)
        add_vec(V_LN2G, upstream * unit)
        add_vec(V_LN2B, upstream)
        scaled = upstream * gain_two
        grad = grad_out + inverse * (
            scaled
            - jnp.mean(scaled, axis=1, keepdims=True)
            - unit * jnp.mean(scaled * unit, axis=1, keepdims=True)
        )
        slots[RES, here, :] = grad
        low = grad.astype(bf16)
        nrm[here, :] = low
        add_vec(V_OB, low.astype(f32))
        return carry

    lax.fori_loop(0, row_tiles, second_back, 0)

    GQ = ACC

    def mixed_back(c, carry):
        cols = pl.ds(pl.multiple_of(c * wide, wide), wide)
        gm[:, cols] = dot_nt(nrm[...], wout[cols, :]).astype(bf16)
        mixed = slots[MIXED, :, cols].astype(bf16)
        wfc1[cols, 3 * D : 4 * D] = dot_tn(mixed, nrm[...]).astype(bf16)
        return carry

    lax.fori_loop(0, D // wide, mixed_back, 0)

    def backward_pair(part, hp, key_ref, key_at, value_at):
        col = pl.multiple_of(hp * 128, 128)
        cols = pl.ds(col, 128)
        step = (1 - part) * PAIRS + hp
        slot = step % RING
        q = qkv[:, cols]
        k = key_ref[:, pl.ds(key_at + col, 128)]
        v = key_ref[:, pl.ds(value_at + col, 128)]
        grad_in = gm[:, cols].astype(f32)
        factor = slots[F_OWN if part == 0 else F_TWIN, :, cols]
        product = grad_in * slots[MIXED, :, cols] * factor
        scaled = (grad_in * factor).astype(bf16)
        q_t = q.T
        scaled_t = scaled.T
        e_copy(e_number(step), slot, False).wait()
        grad_q = None
        grad_k, grad_v = [], []
        for h in range(2):
            delta = jnp.sum(half(product, h), axis=1, keepdims=True)
            e = ering[slot, h]
            grad_probs = dot_nt(scaled, half(v, h))
            grad_scores = (e.astype(f32) * (grad_probs - delta)).astype(bf16)
            term = dot(grad_scores, half(k, h))
            grad_q = term if grad_q is None else grad_q + term
            grad_k.append(dot(q_t[64 * h : 64 * h + 64], grad_scores))
            grad_v.append(dot(scaled_t[64 * h : 64 * h + 64], e))

        @pl.when(step + RING < 2 * PAIRS)
        def _():
            e_copy(e_number(step + RING), slot, False).start()

        key_ref[:, pl.ds(key_at + col, 128)] = jnp.concatenate(grad_k, axis=0).T.astype(bf16)
        key_ref[:, pl.ds(value_at + col, 128)] = jnp.concatenate(grad_v, axis=0).T.astype(bf16)
        if part == 1:
            slots[GQ, :, cols] = grad_q
        else:
            total_q = (slots[GQ, :, cols] + grad_q) * score_scale
            qkv[:, cols] = total_q.astype(bf16)

    pairs_loop(lambda hp: backward_pair(1, hp, kvp, 0, D))

    def partial_out(c, carry):
        cols = pl.ds(pl.multiple_of(c * wide, wide), wide)
        gn_out[:, cols] = dot_nt(kvp[...], wqkv[cols, D : 3 * D]).astype(bf16)
        return carry

    lax.fori_loop(0, D // wide, partial_out, 0)
    send_gn = to_twin(2, gn_out, gn_in)
    send_gn.start()

    pairs_loop(lambda hp: backward_pair(0, hp, qkv, D, 2 * D))

    def weight_own(c, carry):
        cols = pl.ds(pl.multiple_of(c * wide, wide), wide)
        wfc1[:, cols] = dot(nrm_t[:, :rows], qkv[:, cols]).astype(bf16)
        add_vec_cols(V_QB, cols, qkv[:, cols])
        return carry

    def add_vec_cols(kind, cols, values):
        vec_ref[kind : kind + 1, cols] = column_sum(values.astype(f32))

    lax.fori_loop(0, D // wide, weight_own, 0)

    def weight_both(c, carry):
        col = pl.multiple_of(c * wide, wide)
        own = qkv[:, pl.ds(D + col, wide)]
        other = kvp[:, pl.ds(col, wide)]
        joint = jnp.concatenate([own, other], axis=0)
        wfc1[:, pl.ds(D + col, wide)] = dot(nrm_t[...], joint).astype(bf16)
        return carry

    lax.fori_loop(0, 2 * D // wide, weight_both, 0)
    store_qo = pltpu.make_async_copy(wfc1, gqo_hbm, out_sem.at[2])
    store_qo.start()

    def value_sum(c, carry):
        col = pl.multiple_of(c * wide, wide)
        values = qkv[:, pl.ds(2 * D + col, wide)].astype(f32)
        other = kvp[:, pl.ds(D + col, wide)].astype(f32)
        vec_ref[V_VB : V_VB + 1, pl.ds(col, wide)] = column_sum(values + other)
        return carry

    lax.fori_loop(0, D // wide, value_sum, 0)

    def first_back_product(c, carry):
        cols = pl.ds(pl.multiple_of(c * wide, wide), wide)
        slots[GNT, :, cols] = dot_nt(qkv[...], wqkv[cols, :])
        return carry

    lax.fori_loop(0, D // wide, first_back_product, 0)
    send_gn.wait()
    gain_one = row(ln1_gain)

    def first_back(t, carry):
        here = tile(t)
        unit, inverse = unit_of(tok[here, :].astype(f32))
        upstream = slots[GNT, here, :] + gn_in[here, :].astype(f32)
        add_vec(V_LN1G, upstream * unit)
        add_vec(V_LN1B, upstream)
        scaled = upstream * gain_one
        grad = slots[RES, here, :] + inverse * (
            scaled
            - jnp.mean(scaled, axis=1, keepdims=True)
            - unit * jnp.mean(scaled * unit, axis=1, keepdims=True)
        )
        gtok_ref[0, here, :] = grad.astype(bf16)
        return carry

    lax.fori_loop(0, row_tiles, first_back, 0)
    store_fc1.wait()
    store_fc2.wait()
    store_qo.wait()


def block_body(
    tokens,
    lengths,
    padding,
    cotangent,
    ln1_gain,
    ln1_bias,
    w_qkv,
    q_bias,
    v_bias,
    w_out,
    out_bias,
    ln2_gain,
    ln2_bias,
    w_fc1,
    fc1_bias,
    w_fc2,
    fc2_bias,
):
    rows = tokens.shape[1]
    n_dev = lax.axis_size("seq") * lax.axis_size("blk")
    shape = jax.ShapeDtypeStruct
    any_spec = pl.BlockSpec(memory_space=pl.ANY)
    vmem = pl.BlockSpec(memory_space=pltpu.VMEM)
    smem = pl.BlockSpec(memory_space=pltpu.SMEM)
    result, grad_tokens, vec, fb1, gfc1, gfc2, gqo, _ = pl.pallas_call(
        block_kernel,
        name="block",
        out_shape=(
            shape((1, rows, D), bf16),
            shape((1, rows, D), bf16),
            shape((8, D), f32),
            shape((1, FF), f32),
            shape((D, FF), bf16),
            shape((FF, D), bf16),
            shape((D, 4 * D), bf16),
            shape((2 * PAIRS, 2, rows, rows), bf16),
        ),
        in_specs=[
            any_spec, smem, vmem, any_spec, vmem, vmem, any_spec, vmem, vmem,
            any_spec, vmem, vmem, vmem, any_spec, vmem, any_spec, vmem,
        ],
        out_specs=(vmem, vmem, vmem, vmem, any_spec, any_spec, any_spec, any_spec),
        scratch_shapes=[
            pltpu.VMEM((D, 3 * D), bf16),
            pltpu.VMEM((D, D), bf16),
            pltpu.VMEM((D, FF), bf16),
            pltpu.VMEM((FF, D), bf16),
            pltpu.VMEM((rows, D), bf16),
            pltpu.VMEM((rows, D), bf16),
            pltpu.VMEM((rows, D), bf16),
            pltpu.VMEM((rows, D), bf16),
            pltpu.VMEM((D, 2 * rows), bf16),
            pltpu.VMEM((D, rows), bf16),
            pltpu.VMEM((rows, 3 * D), bf16),
            pltpu.VMEM((rows, 2 * D), bf16),
            pltpu.VMEM((rows, D), bf16),
            pltpu.VMEM((rows, rows), f32),
            pltpu.VMEM((RING, 2, rows, rows), bf16),
            pltpu.VMEM((6, rows, D), f32),
            pltpu.VMEM((D, FF), bf16),
            pltpu.VMEM((FF, D), bf16),
            pltpu.VMEM((rows, D), bf16),
            pltpu.VMEM((rows, D), bf16),
            pltpu.VMEM((2, 8, rows), jnp.int32),
            pltpu.SemaphoreType.DMA((6,)),
            pltpu.SemaphoreType.DMA((RING,)),
            pltpu.SemaphoreType.DMA((3,)),
            pltpu.SemaphoreType.DMA((3,)),
            pltpu.SemaphoreType.DMA((3,)),
        ],
        compiler_params=pltpu.CompilerParams(
            collective_id=0, has_side_effects=True, vmem_limit_bytes=VMEM_LIMIT
        ),
        cost_estimate=pl.CostEstimate(
            flops=30 * 10**9, bytes_accessed=60 * 10**6, transcendentals=10**7
        ),
    )(
        tokens, lengths, padding, cotangent, ln1_gain, ln1_bias, w_qkv, q_bias, v_bias,
        w_out, out_bias, ln2_gain, ln2_bias, w_fc1, fc1_bias, w_fc2, fc2_bias,
    )
    small = jnp.concatenate(
        [vec[k].reshape(n_dev, -1) for k in range(8)] + [fb1.reshape(n_dev, -1)], axis=1
    )
    sum_fc2 = scatter_sum(gfc2)
    sum_fc1 = scatter_sum(gfc1)
    sum_qo = scatter_sum(gqo)
    small = scatter_stages(small, stage_orders()[0])[0]
    part = D // n_dev
    one = [small[k * part : (k + 1) * part] for k in range(8)]
    return (
        result,
        grad_tokens,
        one[0],
        one[1],
        sum_qo[:, : 3 * D],
        one[2],
        one[3],
        sum_qo[:, 3 * D :],
        one[4],
        one[5],
        one[6],
        sum_fc1,
        small[8 * part :],
        sum_fc2,
        one[7],
    )


VMEM_LIMIT = 62 * 2**20


def solution(mesh):
    in_specs = (
        P("seq", "blk", None),
        P("seq", None),
        P("seq", "blk"),
        P("seq", "blk", None),
        P(),
        P(),
        P(),
        P(),
        P(),
        P(),
        P(),
        P(),
        P(),
        P(),
        P(),
        P(),
        P(),
    )
    out_specs = (
        P("seq", "blk", None),
        P("seq", "blk", None),
        P(("seq", "blk")),
        P(("seq", "blk")),
        P(("seq", "blk"), None),
        P(("seq", "blk")),
        P(("seq", "blk")),
        P(("seq", "blk"), None),
        P(("seq", "blk")),
        P(("seq", "blk")),
        P(("seq", "blk")),
        P(("seq", "blk"), None),
        P(("seq", "blk")),
        P(("seq", "blk"), None),
        P(("seq", "blk")),
    )
    step = block_body if fits(mesh) else body
    return jax.shard_map(step, mesh=mesh, in_specs=in_specs, out_specs=out_specs, check_vma=False)
```

profile of v0, /device:TPU:0, one launch (start us, length us, event | category | flops | bytes accessed | tf_op | source)
XLA Modules:
  0.0 221.2 jit_solution(17822685225386452158)
XLA Ops:
  0.7 86.7 %block.1 = (bf16[1,512,768]{2,1,0:T(8,128)(2,1)}, bf16[1,512,768]{2,1,0:T(8,128)(2,1)}, f32[8,768]{1,0:T(8,128)}, f32[1,3072]{1,0:T(1,128)}, bf16[768,3072]{1,0:...) custom-call(bf16[1,512,768]{2,1,0:T(8,128)(2,1)} %tok_hbm.1, ...), custom_call_target="tpu_custom_call" | custom-call | flops 30000001024 | bytes 60000000 | tf_op jit(solution)/shard_map/block/pallas_call | solution.py:877
  87.4 1.3 slice_reduce_fusion
  90.0 1.4 reduce.19
  92.4 2.7 %fusion.6 = (bf16[32,24,1536]{2,1,0:T(8,128)(2,1)S(1)}, bf16[32,24,1536]{2,1,0:T(8,128)(2,1)S(1)}) fusion(bf16[32,24,3072]{2,1,0:T(8,128)(2,1)} %bitcast.53), kind=kLoop, calls=%fused_computation.96 | loop fusion | bytes 9437184 | tf_op jit(solution)/shard_map/slice | solution.py:112
  95.1 1.2 constant_dynamic-slice_fusion.24
  96.9 1.2 constant_dynamic-slice_fusion.29
  98.6 2.7 %fusion.5 = (bf16[32,24,1536]{2,1,0:T(8,128)(2,1)S(1)}, bf16[32,24,1536]{2,1,0:T(8,128)(2,1)S(1)}) fusion(bf16[32,24,3072]{2,1,0:T(8,128)(2,1)} %bitcast.52), kind=kLoop, calls=%fused_computation.95 | loop fusion | bytes 9437184 | tf_op jit(solution)/shard_map/slice | solution.py:112
  101.4 1.3 copy-done.2
  102.7 0.8 dynamic-slice_add_fusion
  104.1 1.5 collective-permute-start.1
  105.6 1.1 constant_dynamic-slice_fusion.19
  107.0 0.9 collective-permute-done.1
  107.9 0.7 fusion
  109.2 0.6 collective-permute-start.2
  109.9 5.0 %fusion.4 = (bf16[32,96,384]{2,1,0:T(8,128)(2,1)}, bf16[32,96,384]{2,1,0:T(8,128)(2,1)}) fusion(bf16[32,96,768]{2,1,0:T(8,128)(2,1)} %bitcast.51), kind=kLoop, calls=%fused_computation.94 | loop fusion | bytes 9437184 | tf_op jit(solution)/shard_map/slice | solution.py:112
  114.9 0.7 fusion.1
  116.2 1.4 collective-permute-start.3
  117.7 2.5 %constant_dynamic-slice_fusion.4 = bf16[2,2,2,1,2,96,384]{6,5,4,3,2,1,0:T(8,128)(2,1)} fusion(bf16[2,2,2,2,2,96,384]{6,5,4,3,2,1,0:T(8,128)(2,1)} %bitcast.49, s32[]{:T(128)S(6)} %select_n.21), kind=kLoop, calls=%fused_computation.38 | loop fusion | bytes 2359300 | tf_op jit(solution)/shard_map/dynamic_slice | solution.py:98
  120.2 2.6 %collective-permute-start.4 = (f32[1,1,1,1,1,288]{5,4,3,2,1,0:T(1,128)S(1)}, f32[1,1,1,1,1,288]{5,4,3,2,1,0:T(1,128)S(1)}, u32[]{:S(2)}, u32[]{:S(2)}) collective-permute-start(f32[1,1,1,1,1,288]{5,4,3,2,1,0:T(1,128)S(1)} %constant_dynamic-slice_fusion.30), channel_id=1, source_target_pairs={{0,16},{1,17},{2,18},{3,19},{4,20},{5,21},{6,22},{7,23},{8,24},{9,... | collective-permute-start | bytes 3464 | tf_op jit(solution)/shard_map/ppermute | solution.py:101
  122.8 2.4 %constant_dynamic-slice_fusion.9 = bf16[2,2,2,1,2,96,384]{6,5,4,3,2,1,0:T(8,128)(2,1)} fusion(bf16[2,2,2,2,2,96,384]{6,5,4,3,2,1,0:T(8,128)(2,1)} %bitcast.47, s32[]{:T(128)S(6)} %select_n.21), kind=kLoop, calls=%fused_computation.43 | loop fusion | bytes 2359300 | tf_op jit(solution)/shard_map/dynamic_slice | solution.py:98
  127.0 2.1 add_convert_fusion.4
  129.2 1.7 collective-permute-start.11
  130.8 1.8 add_convert_fusion.5
  132.7 1.6 collective-permute-start.6
  134.3 1.6 add_convert_fusion.2
  136.5 1.8 add_convert_fusion.3
  139.3 1.7 collective-permute-start.31
  141.4 4.1 %collective-permute-done.11 = bf16[2,2,2,1,1,24,1536]{6,5,4,3,2,1,0:T(8,128)(2,1)S(1)} collective-permute-done((bf16[2,2,2,1,1,24,1536]{6,5,4,3,2,1,0:T(8,128)(2,1)S(1)}, bf16[2,2,2,1,1,24,1536]{6,5,4,3,2,1,0:T(8,128)(2,1)S(1)}, u32[]{:S(2)}, u32[]{:S(2)}) %collective-permute-start.11) | collective-permute-done | bytes 589856 | tf_op jit(solution)/shard_map/ppermute | solution.py:101
  145.4 1.6 collective-permute-start.26
  147.2 1.8 collective-permute-done.6
  149.0 1.5 collective-permute-start.12
  150.7 7.4 %collective-permute-done.21 = bf16[2,2,2,1,1,24,1536]{6,5,4,3,2,1,0:T(8,128)(2,1)S(1)} collective-permute-done((bf16[2,2,2,1,1,24,1536]{6,5,4,3,2,1,0:T(8,128)(2,1)S(1)}, bf16[2,2,2,1,1,24,1536]{6,5,4,3,2,1,0:T(8,128)(2,1)S(1)}, u32[]{:S(2)}, u32[]{:S(2)}) %collective-permute-start.21) | collective-permute-done | bytes 589856 | tf_op jit(solution)/shard_map/ppermute | solution.py:101
  158.1 1.6 collective-permute-start.7
  159.9 1.8 collective-permute-done.16
  161.6 1.5 collective-permute-start.22
  163.3 7.4 %collective-permute-done.31 = bf16[2,2,2,1,1,96,384]{6,5,4,3,2,1,0:T(8,128)(2,1)S(1)} collective-permute-done((bf16[2,2,2,1,1,96,384]{6,5,4,3,2,1,0:T(8,128)(2,1)S(1)}, bf16[2,2,2,1,1,96,384]{6,5,4,3,2,1,0:T(8,128)(2,1)S(1)}, u32[]{:S(2)}, u32[]{:S(2)}) %collective-permute-start.31) | collective-permute-done | bytes 589856 | tf_op jit(solution)/shard_map/ppermute | solution.py:101
  170.7 1.6 collective-permute-start.17
  172.5 1.7 collective-permute-done.26
  174.3 1.5 collective-permute-start.32
  176.0 4.6 %collective-permute-done.12 = bf16[2,2,1,1,1,24,1536]{6,5,4,3,2,1,0:T(8,128)(2,1)S(1)} collective-permute-done((bf16[2,2,1,1,1,24,1536]{6,5,4,3,2,1,0:T(8,128)(2,1)S(1)}, bf16[2,2,1,1,1,24,1536]{6,5,4,3,2,1,0:T(8,128)(2,1)S(1)}, u32[]{:S(2)}, u32[]{:S(2)}) %collective-permute-start.12) | collective-permute-done | bytes 294944 | tf_op jit(solution)/shard_map/ppermute | solution.py:101
  181.1 1.2 collective-permute-start.13
  182.4 4.5 %collective-permute-done.22 = bf16[2,2,1,1,1,24,1536]{6,5,4,3,2,1,0:T(8,128)(2,1)S(1)} collective-permute-done((bf16[2,2,1,1,1,24,1536]{6,5,4,3,2,1,0:T(8,128)(2,1)S(1)}, bf16[2,2,1,1,1,24,1536]{6,5,4,3,2,1,0:T(8,128)(2,1)S(1)}, u32[]{:S(2)}, u32[]{:S(2)}) %collective-permute-start.22) | collective-permute-done | bytes 294944 | tf_op jit(solution)/shard_map/ppermute | solution.py:101
  186.9 1.1 collective-permute-start.8
  188.1 1.0 collective-permute-start.23
  189.2 2.8 %collective-permute-done.32 = bf16[2,2,1,1,1,96,384]{6,5,4,3,2,1,0:T(8,128)(2,1)S(1)} collective-permute-done((bf16[2,2,1,1,1,96,384]{6,5,4,3,2,1,0:T(8,128)(2,1)S(1)}, bf16[2,2,1,1,1,96,384]{6,5,4,3,2,1,0:T(8,128)(2,1)S(1)}, u32[]{:S(2)}, u32[]{:S(2)}) %collective-permute-start.32) | collective-permute-done | bytes 294944 | tf_op jit(solution)/shard_map/ppermute | solution.py:101
  192.0 1.1 collective-permute-start.18
  193.2 1.0 collective-permute-start.33
  194.3 1.2 collective-permute-start.28
  195.6 2.1 collective-permute-start.14
  197.8 0.9 collective-permute-start.9
  198.8 3.2 %collective-permute-done.18 = bf16[2,1,1,1,1,24,1536]{6,5,4,3,2,1,0:T(8,128)(2,1)S(1)} collective-permute-done((bf16[2,1,1,1,1,24,1536]{6,5,4,3,2,1,0:T(8,128)(2,1)S(1)}, bf16[2,1,1,1,1,24,1536]{6,5,4,3,2,1,0:T(8,128)(2,1)S(1)}, u32[]{:S(2)}, u32[]{:S(2)}) %collective-permute-start.18) | collective-permute-done | bytes 147488 | tf_op jit(solution)/shard_map/ppermute | solution.py:101
  201.9 1.0 collective-permute-start.24
  203.0 3.2 %collective-permute-done.33 = bf16[2,1,1,1,1,96,384]{6,5,4,3,2,1,0:T(8,128)(2,1)S(1)} collective-permute-done((bf16[2,1,1,1,1,96,384]{6,5,4,3,2,1,0:T(8,128)(2,1)S(1)}, bf16[2,1,1,1,1,96,384]{6,5,4,3,2,1,0:T(8,128)(2,1)S(1)}, u32[]{:S(2)}, u32[]{:S(2)}) %collective-permute-start.33) | collective-permute-done | bytes 147488 | tf_op jit(solution)/shard_map/ppermute | solution.py:101
  206.3 0.7 collective-permute-start.19
  207.0 1.0 collective-permute-done.28
  208.0 1.3 collective-permute-start.34
  209.4 1.7 collective-permute-start.29
  211.2 3.4 %collective-permute-done.24 = bf16[1,1,1,1,1,24,1536]{6,5,4,3,2,1,0:T(8,128)(2,1)S(1)} collective-permute-done((bf16[1,1,1,1,1,24,1536]{6,5,4,3,2,1,0:T(8,128)(2,1)S(1)}, bf16[1,1,1,1,1,24,1536]{6,5,4,3,2,1,0:T(8,128)(2,1)S(1)}, u32[]{:S(2)}, u32[]{:S(2)}) %collective-permute-start.24) | collective-permute-done | bytes 73760 | tf_op jit(solution)/shard_map/ppermute | solution.py:101
  214.6 0.7 pad_maximum_fusion.2
  215.3 1.6 collective-permute-done.19
  217.0 0.7 pad_maximum_fusion
  218.7 0.7 pad_maximum_fusion.1
  219.5 0.9 copy.34
  220.4 0.9 copy.35
  (127 shorter events, 12.9 us)
Async XLA Ops:
  91.7 3.3 %copy-start.9 = (f32[2,2,2,2,2,288]{5,4,3,2,1,0:T(2,128)}, f32[2,2,2,2,2,288]{5,4,3,2,1,0:T(2,128)S(1)}, u32[]{:S(2)}) copy-start(f32[2,2,2,2,2,288]{5,4,3,2,1,0:T(2,128)S(1)} %concatenate.40) | copy-start | bytes 110596
  92.4 10.4 %collective-permute-start = (f32[2,2,2,1,2,288]{5,4,3,2,1,0:T(2,128)}, f32[2,2,2,1,2,288]{5,4,3,2,1,0:T(2,128)}, u32[]{:S(2)}, u32[]{:S(2)}) collective-permute-start(f32[2,2,2,1,2,288]{5,4,3,2,1,0:T(2,128)} %constant_dynamic-slice_fusion.38), channel_id=1, source_target_pairs={{0,2},{1,3},{2,0},{3,1},{4,6},{5,7},{6,4},{7,5},{8,10},{9,11},{10,... | collective-permute-start | bytes 55304 | tf_op jit(solution)/shard_map/ppermute | solution.py:101
  95.1 1.8 copy-start
  95.1 6.2 %copy-start.4 = (bf16[32,24,1536]{2,1,0:T(8,128)(2,1)}, bf16[32,24,1536]{2,1,0:T(8,128)(2,1)S(1)}, u32[]{:S(2)}) copy-start(bf16[32,24,1536]{2,1,0:T(8,128)(2,1)S(1)} %get-tuple-element.42) | copy-start | bytes 7077892
  96.3 30.1 %collective-permute-start.10 = (bf16[2,2,2,1,2,24,1536]{6,5,4,3,2,1,0:T(8,128)(2,1)}, bf16[2,2,2,1,2,24,1536]{6,5,4,3,2,1,0:T(8,128)(2,1)}, u32[]{:S(2)}, u32[]{:S(2)}) collective-permute-start(bf16[2,2,2,1,2,24,1536]{6,5,4,3,2,1,0:T(8,128)(2,1)} %constant_dynamic-slice_fusion.24), channel_id=1, source_target_pairs={{0,2},{1,3},{2,0},{3,1},{4,6},{5,7},{6,4},{7,5},{8,10},{9,11},{10,... | collective-permute-start | bytes 3538952 | tf_op jit(solution)/shard_map/ppermute | solution.py:101
  98.1 31.1 %collective-permute-start.5 = (bf16[2,2,2,1,2,24,1536]{6,5,4,3,2,1,0:T(8,128)(2,1)}, bf16[2,2,2,1,2,24,1536]{6,5,4,3,2,1,0:T(8,128)(2,1)}, u32[]{:S(2)}, u32[]{:S(2)}) collective-permute-start(bf16[2,2,2,1,2,24,1536]{6,5,4,3,2,1,0:T(8,128)(2,1)} %constant_dynamic-slice_fusion.29), channel_id=1, source_target_pairs={{0,2},{1,3},{2,0},{3,1},{4,6},{5,7},{6,4},{7,5},{8,10},{9,11},{10,... | collective-permute-start | bytes 3538952 | tf_op jit(solution)/shard_map/ppermute | solution.py:101
  101.3 1.4 copy-start.2
  102.7 30.0 %collective-permute-start.20 = (bf16[2,2,2,1,2,24,1536]{6,5,4,3,2,1,0:T(8,128)(2,1)S(1)}, bf16[2,2,2,1,2,24,1536]{6,5,4,3,2,1,0:T(8,128)(2,1)}, u32[]{:S(2)}, u32[]{:S(2)}) collective-permute-start(bf16[2,2,2,1,2,24,1536]{6,5,4,3,2,1,0:T(8,128)(2,1)S(1)} %constant_dynamic-slice_fusion.14), channel_id=1, source_target_pairs={{0,2},{1,3},{2,0},{3,1},{4,6},{5,7},{6,4},{7,5},{8,10},{9,11},{10,... | collective-permute-start | bytes 3538952 | tf_op jit(solution)/shard_map/ppermute | solution.py:101
  103.5 0.6 copy-start.10
  104.1 3.8 %collective-permute-start.1 = (f32[2,2,1,1,2,288]{5,4,3,2,1,0:T(2,128)S(1)}, f32[2,2,1,1,2,288]{5,4,3,2,1,0:T(2,128)}, u32[]{:S(2)}, u32[]{:S(2)}) collective-permute-start(f32[2,2,1,1,2,288]{5,4,3,2,1,0:T(2,128)S(1)} %constant_dynamic-slice_fusion.36), channel_id=1, source_target_pairs={{0,4},{1,5},{2,6},{3,7},{4,0},{5,1},{6,2},{7,3},{8,12},{9,13},{10,... | collective-permute-start | bytes 27656 | tf_op jit(solution)/shard_map/ppermute | solution.py:101
  106.7 29.2 %collective-permute-start.15 = (bf16[2,2,2,1,2,24,1536]{6,5,4,3,2,1,0:T(8,128)(2,1)}, bf16[2,2,2,1,2,24,1536]{6,5,4,3,2,1,0:T(8,128)(2,1)}, u32[]{:S(2)}, u32[]{:S(2)}) collective-permute-start(bf16[2,2,2,1,2,24,1536]{6,5,4,3,2,1,0:T(8,128)(2,1)} %constant_dynamic-slice_fusion.19), channel_id=1, source_target_pairs={{0,2},{1,3},{2,0},{3,1},{4,6},{5,7},{6,4},{7,5},{8,10},{9,11},{10,... | collective-permute-start | bytes 3538952 | tf_op jit(solution)/shard_map/ppermute | solution.py:101
  109.2 5.7 %collective-permute-start.2 = (f32[2,2,1,1,1,288]{5,4,3,2,1,0:T(1,128)}, f32[2,2,1,1,1,288]{5,4,3,2,1,0:T(1,128)}, u32[]{:S(2)}, u32[]{:S(2)}) collective-permute-start(f32[2,2,1,1,1,288]{5,4,3,2,1,0:T(1,128)} %constant_dynamic-slice_fusion.34), channel_id=1, source_target_pairs={{0,1},{1,0},{2,3},{3,2},{4,5},{5,4},{6,7},{7,6},{8,9},{9,8},{10,11... | collective-permute-start | bytes 13832 | tf_op jit(solution)/shard_map/ppermute | solution.py:101
  115.6 0.6 copy-start.11
  116.2 3.9 %collective-permute-start.3 = (f32[2,1,1,1,1,288]{5,4,3,2,1,0:T(1,128)S(1)}, f32[2,1,1,1,1,288]{5,4,3,2,1,0:T(1,128)S(1)}, u32[]{:S(2)}, u32[]{:S(2)}) collective-permute-start(f32[2,1,1,1,1,288]{5,4,3,2,1,0:T(1,128)S(1)} %constant_dynamic-slice_fusion.32), channel_id=1, source_target_pairs={{0,8},{1,9},{2,10},{3,11},{4,12},{5,13},{6,14},{7,15},{8,0},{9,1},... | collective-permute-start | bytes 6920 | tf_op jit(solution)/shard_map/ppermute | solution.py:101
  117.7 2.5 %copy-start.12 = (f32[2,2,1,1,1,288]{5,4,3,2,1,0:T(1,128)S(1)}, f32[2,2,1,1,1,288]{5,4,3,2,1,0:T(1,128)}, u32[]{:S(2)}) copy-start(f32[2,2,1,1,1,288]{5,4,3,2,1,0:T(1,128)} %copy-done.11) | copy-start | bytes 13828
  120.2 5.0 %collective-permute-start.4 = (f32[1,1,1,1,1,288]{5,4,3,2,1,0:T(1,128)S(1)}, f32[1,1,1,1,1,288]{5,4,3,2,1,0:T(1,128)S(1)}, u32[]{:S(2)}, u32[]{:S(2)}) collective-permute-start(f32[1,1,1,1,1,288]{5,4,3,2,1,0:T(1,128)S(1)} %constant_dynamic-slice_fusion.30), channel_id=1, source_target_pairs={{0,16},{1,17},{2,18},{3,19},{4,20},{5,21},{6,22},{7,23},{8,24},{9,... | collective-permute-start | bytes 3464 | tf_op jit(solution)/shard_map/ppermute | solution.py:101
  125.2 13.1 %collective-permute-start.30 = (bf16[2,2,2,1,2,96,384]{6,5,4,3,2,1,0:T(8,128)(2,1)}, bf16[2,2,2,1,2,96,384]{6,5,4,3,2,1,0:T(8,128)(2,1)S(1)}, u32[]{:S(2)}, u32[]{:S(2)}) collective-permute-start(bf16[2,2,2,1,2,96,384]{6,5,4,3,2,1,0:T(8,128)(2,1)} %constant_dynamic-slice_fusion.4), channel_id=1, source_target_pairs={{0,2},{1,3},{2,0},{3,1},{4,6},{5,7},{6,4},{7,5},{8,10},{9,11},{10,... | collective-permute-start | bytes 3538952 | tf_op jit(solution)/shard_map/ppermute | solution.py:101
  126.4 12.9 %collective-permute-start.25 = (bf16[2,2,2,1,2,96,384]{6,5,4,3,2,1,0:T(8,128)(2,1)}, bf16[2,2,2,1,2,96,384]{6,5,4,3,2,1,0:T(8,128)(2,1)S(1)}, u32[]{:S(2)}, u32[]{:S(2)}) collective-permute-start(bf16[2,2,2,1,2,96,384]{6,5,4,3,2,1,0:T(8,128)(2,1)} %constant_dynamic-slice_fusion.9), channel_id=1, source_target_pairs={{0,2},{1,3},{2,0},{3,1},{4,6},{5,7},{6,4},{7,5},{8,10},{9,11},{10,... | collective-permute-start | bytes 3538952 | tf_op jit(solution)/shard_map/ppermute | solution.py:101
  127.0 3.9 %copy-start.1 = (bf16[32,24,1536]{2,1,0:T(8,128)(2,1)S(1)}, bf16[32,24,1536]{2,1,0:T(8,128)(2,1)}, u32[]{:S(2)}) copy-start(bf16[32,24,1536]{2,1,0:T(8,128)(2,1)} %copy-done) | copy-start | bytes 7077892
  129.2 16.3 %collective-permute-start.11 = (bf16[2,2,2,1,1,24,1536]{6,5,4,3,2,1,0:T(8,128)(2,1)S(1)}, bf16[2,2,2,1,1,24,1536]{6,5,4,3,2,1,0:T(8,128)(2,1)S(1)}, u32[]{:S(2)}, u32[]{:S(2)}) collective-permute-start(bf16[2,2,2,1,1,24,1536]{6,5,4,3,2,1,0:T(8,128)(2,1)S(1)} %constant_dynamic-slice_fusion.23), channel_id=1, source_target_pairs={{0,1},{1,0},{2,3},{3,2},{4,5},{5,4},{6,7},{7,6},{8,9},{9,8},{10,11... | collective-permute-start | bytes 1769480 | tf_op jit(solution)/shard_map/ppermute | solution.py:101
  130.8 3.4 %copy-start.3 = (bf16[32,24,1536]{2,1,0:T(8,128)(2,1)S(1)}, bf16[32,24,1536]{2,1,0:T(8,128)(2,1)}, u32[]{:S(2)}) copy-start(bf16[32,24,1536]{2,1,0:T(8,128)(2,1)} %copy-done.2) | copy-start | bytes 7077892
  132.7 16.3 %collective-permute-start.6 = (bf16[2,2,1,1,2,24,1536]{6,5,4,3,2,1,0:T(8,128)(2,1)S(1)}, bf16[2,2,1,1,2,24,1536]{6,5,4,3,2,1,0:T(8,128)(2,1)S(1)}, u32[]{:S(2)}, u32[]{:S(2)}) collective-permute-start(bf16[2,2,1,1,2,24,1536]{6,5,4,3,2,1,0:T(8,128)(2,1)S(1)} %constant_dynamic-slice_fusion.28), channel_id=1, source_target_pairs={{0,4},{1,5},{2,6},{3,7},{4,0},{5,1},{6,2},{7,3},{8,12},{9,13},{10,... | collective-permute-start | bytes 1769480 | tf_op jit(solution)/shard_map/ppermute | solution.py:101
  135.9 22.1 %collective-permute-start.21 = (bf16[2,2,2,1,1,24,1536]{6,5,4,3,2,1,0:T(8,128)(2,1)S(1)}, bf16[2,2,2,1,1,24,1536]{6,5,4,3,2,1,0:T(8,128)(2,1)S(1)}, u32[]{:S(2)}, u32[]{:S(2)}) collective-permute-start(bf16[2,2,2,1,1,24,1536]{6,5,4,3,2,1,0:T(8,128)(2,1)S(1)} %constant_dynamic-slice_fusion.13), channel_id=1, source_target_pairs={{0,1},{1,0},{2,3},{3,2},{4,5},{5,4},{6,7},{7,6},{8,9},{9,8},{10,11... | collective-permute-start | bytes 1769480 | tf_op jit(solution)/shard_map/ppermute | solution.py:101
  136.5 2.4 %copy-start.6 = (bf16[32,96,384]{2,1,0:T(8,128)(2,1)S(1)}, bf16[32,96,384]{2,1,0:T(8,128)(2,1)}, u32[]{:S(2)}) copy-start(bf16[32,96,384]{2,1,0:T(8,128)(2,1)} %get-tuple-element.38) | copy-start | bytes 7077892
  138.4 23.3 %collective-permute-start.16 = (bf16[2,2,1,1,2,24,1536]{6,5,4,3,2,1,0:T(8,128)(2,1)S(1)}, bf16[2,2,1,1,2,24,1536]{6,5,4,3,2,1,0:T(8,128)(2,1)S(1)}, u32[]{:S(2)}, u32[]{:S(2)}) collective-permute-start(bf16[2,2,1,1,2,24,1536]{6,5,4,3,2,1,0:T(8,128)(2,1)S(1)} %constant_dynamic-slice_fusion.18), channel_id=1, source_target_pairs={{0,4},{1,5},{2,6},{3,7},{4,0},{5,1},{6,2},{7,3},{8,12},{9,13},{10,... | collective-permute-start | bytes 1769480 | tf_op jit(solution)/shard_map/ppermute | solution.py:101
  138.9 2.1 copy-start.5
  139.3 31.4 %collective-permute-start.31 = (bf16[2,2,2,1,1,96,384]{6,5,4,3,2,1,0:T(8,128)(2,1)S(1)}, bf16[2,2,2,1,1,96,384]{6,5,4,3,2,1,0:T(8,128)(2,1)S(1)}, u32[]{:S(2)}, u32[]{:S(2)}) collective-permute-start(bf16[2,2,2,1,1,96,384]{6,5,4,3,2,1,0:T(8,128)(2,1)S(1)} %constant_dynamic-slice_fusion.3), channel_id=1, source_target_pairs={{0,1},{1,0},{2,3},{3,2},{4,5},{5,4},{6,7},{7,6},{8,9},{9,8},{10,11... | collective-permute-start | bytes 1769480 | tf_op jit(solution)/shard_map/ppermute | solution.py:101
  145.4 28.8 %collective-permute-start.26 = (bf16[2,2,1,1,2,96,384]{6,5,4,3,2,1,0:T(8,128)(2,1)S(1)}, bf16[2,2,1,1,2,96,384]{6,5,4,3,2,1,0:T(8,128)(2,1)S(1)}, u32[]{:S(2)}, u32[]{:S(2)}) collective-permute-start(bf16[2,2,1,1,2,96,384]{6,5,4,3,2,1,0:T(8,128)(2,1)S(1)} %constant_dynamic-slice_fusion.8), channel_id=1, source_target_pairs={{0,4},{1,5},{2,6},{3,7},{4,0},{5,1},{6,2},{7,3},{8,12},{9,13},{10,... | collective-permute-start | bytes 1769480 | tf_op jit(solution)/shard_map/ppermute | solution.py:101
  149.0 31.6 %collective-permute-start.12 = (bf16[2,2,1,1,1,24,1536]{6,5,4,3,2,1,0:T(8,128)(2,1)S(1)}, bf16[2,2,1,1,1,24,1536]{6,5,4,3,2,1,0:T(8,128)(2,1)S(1)}, u32[]{:S(2)}, u32[]{:S(2)}) collective-permute-start(bf16[2,2,1,1,1,24,1536]{6,5,4,3,2,1,0:T(8,128)(2,1)S(1)} %constant_dynamic-slice_fusion.22), channel_id=1, source_target_pairs={{0,4},{1,5},{2,6},{3,7},{4,0},{5,1},{6,2},{7,3},{8,12},{9,13},{10,... | collective-permute-start | bytes 884744 | tf_op jit(solution)/shard_map/ppermute | solution.py:101
  158.1 23.1 %collective-permute-start.7 = (bf16[2,2,1,1,1,24,1536]{6,5,4,3,2,1,0:T(8,128)(2,1)S(1)}, bf16[2,2,1,1,1,24,1536]{6,5,4,3,2,1,0:T(8,128)(2,1)S(1)}, u32[]{:S(2)}, u32[]{:S(2)}) collective-permute-start(bf16[2,2,1,1,1,24,1536]{6,5,4,3,2,1,0:T(8,128)(2,1)S(1)} %constant_dynamic-slice_fusion.27), channel_id=1, source_target_pairs={{0,1},{1,0},{2,3},{3,2},{4,5},{5,4},{6,7},{7,6},{8,9},{9,8},{10,11... | collective-permute-start | bytes 884744 | tf_op jit(solution)/shard_map/ppermute | solution.py:101
  161.6 25.3 %collective-permute-start.22 = (bf16[2,2,1,1,1,24,1536]{6,5,4,3,2,1,0:T(8,128)(2,1)S(1)}, bf16[2,2,1,1,1,24,1536]{6,5,4,3,2,1,0:T(8,128)(2,1)S(1)}, u32[]{:S(2)}, u32[]{:S(2)}) collective-permute-start(bf16[2,2,1,1,1,24,1536]{6,5,4,3,2,1,0:T(8,128)(2,1)S(1)} %constant_dynamic-slice_fusion.12), channel_id=1, source_target_pairs={{0,4},{1,5},{2,6},{3,7},{4,0},{5,1},{6,2},{7,3},{8,12},{9,13},{10,... | collective-permute-start | bytes 884744 | tf_op jit(solution)/shard_map/ppermute | solution.py:101
  170.7 17.4 %collective-permute-start.17 = (bf16[2,2,1,1,1,24,1536]{6,5,4,3,2,1,0:T(8,128)(2,1)S(1)}, bf16[2,2,1,1,1,24,1536]{6,5,4,3,2,1,0:T(8,128)(2,1)S(1)}, u32[]{:S(2)}, u32[]{:S(2)}) collective-permute-start(bf16[2,2,1,1,1,24,1536]{6,5,4,3,2,1,0:T(8,128)(2,1)S(1)} %constant_dynamic-slice_fusion.17), channel_id=1, source_target_pairs={{0,1},{1,0},{2,3},{3,2},{4,5},{5,4},{6,7},{7,6},{8,9},{9,8},{10,11... | collective-permute-start | bytes 884744 | tf_op jit(solution)/shard_map/ppermute | solution.py:101
  174.3 17.7 %collective-permute-start.32 = (bf16[2,2,1,1,1,96,384]{6,5,4,3,2,1,0:T(8,128)(2,1)S(1)}, bf16[2,2,1,1,1,96,384]{6,5,4,3,2,1,0:T(8,128)(2,1)S(1)}, u32[]{:S(2)}, u32[]{:S(2)}) collective-permute-start(bf16[2,2,1,1,1,96,384]{6,5,4,3,2,1,0:T(8,128)(2,1)S(1)} %constant_dynamic-slice_fusion.2), channel_id=1, source_target_pairs={{0,4},{1,5},{2,6},{3,7},{4,0},{5,1},{6,2},{7,3},{8,12},{9,13},{10,... | collective-permute-start | bytes 884744 | tf_op jit(solution)/shard_map/ppermute | solution.py:101
  180.6 12.6 %collective-permute-start.27 = (bf16[2,2,1,1,1,96,384]{6,5,4,3,2,1,0:T(8,128)(2,1)S(1)}, bf16[2,2,1,1,1,96,384]{6,5,4,3,2,1,0:T(8,128)(2,1)S(1)}, u32[]{:S(2)}, u32[]{:S(2)}) collective-permute-start(bf16[2,2,1,1,1,96,384]{6,5,4,3,2,1,0:T(8,128)(2,1)S(1)} %constant_dynamic-slice_fusion.7), channel_id=1, source_target_pairs={{0,1},{1,0},{2,3},{3,2},{4,5},{5,4},{6,7},{7,6},{8,9},{9,8},{10,11... | collective-permute-start | bytes 884744 | tf_op jit(solution)/shard_map/ppermute | solution.py:101
  181.1 13.2 %collective-permute-start.13 = (bf16[2,1,1,1,1,24,1536]{6,5,4,3,2,1,0:T(8,128)(2,1)S(1)}, bf16[2,1,1,1,1,24,1536]{6,5,4,3,2,1,0:T(8,128)(2,1)S(1)}, u32[]{:S(2)}, u32[]{:S(2)}) collective-permute-start(bf16[2,1,1,1,1,24,1536]{6,5,4,3,2,1,0:T(8,128)(2,1)S(1)} %constant_dynamic-slice_fusion.21), channel_id=1, source_target_pairs={{0,8},{1,9},{2,10},{3,11},{4,12},{5,13},{6,14},{7,15},{8,0},{9,1},... | collective-permute-start | bytes 442376 | tf_op jit(solution)/shard_map/ppermute | solution.py:101
  186.9 8.7 %collective-permute-start.8 = (bf16[2,1,1,1,1,24,1536]{6,5,4,3,2,1,0:T(8,128)(2,1)S(1)}, bf16[2,1,1,1,1,24,1536]{6,5,4,3,2,1,0:T(8,128)(2,1)S(1)}, u32[]{:S(2)}, u32[]{:S(2)}) collective-permute-start(bf16[2,1,1,1,1,24,1536]{6,5,4,3,2,1,0:T(8,128)(2,1)S(1)} %constant_dynamic-slice_fusion.26), channel_id=1, source_target_pairs={{0,8},{1,9},{2,10},{3,11},{4,12},{5,13},{6,14},{7,15},{8,0},{9,1},... | collective-permute-start | bytes 442376 | tf_op jit(solution)/shard_map/ppermute | solution.py:101
  188.1 9.6 %collective-permute-start.23 = (bf16[2,1,1,1,1,24,1536]{6,5,4,3,2,1,0:T(8,128)(2,1)S(1)}, bf16[2,1,1,1,1,24,1536]{6,5,4,3,2,1,0:T(8,128)(2,1)S(1)}, u32[]{:S(2)}, u32[]{:S(2)}) collective-permute-start(bf16[2,1,1,1,1,24,1536]{6,5,4,3,2,1,0:T(8,128)(2,1)S(1)} %constant_dynamic-slice_fusion.11), channel_id=1, source_target_pairs={{0,8},{1,9},{2,10},{3,11},{4,12},{5,13},{6,14},{7,15},{8,0},{9,1},... | collective-permute-start | bytes 442376 | tf_op jit(solution)/shard_map/ppermute | solution.py:101
  192.0 9.9 %collective-permute-start.18 = (bf16[2,1,1,1,1,24,1536]{6,5,4,3,2,1,0:T(8,128)(2,1)S(1)}, bf16[2,1,1,1,1,24,1536]{6,5,4,3,2,1,0:T(8,128)(2,1)S(1)}, u32[]{:S(2)}, u32[]{:S(2)}) collective-permute-start(bf16[2,1,1,1,1,24,1536]{6,5,4,3,2,1,0:T(8,128)(2,1)S(1)} %constant_dynamic-slice_fusion.16), channel_id=1, source_target_pairs={{0,8},{1,9},{2,10},{3,11},{4,12},{5,13},{6,14},{7,15},{8,0},{9,1},... | collective-permute-start | bytes 442376 | tf_op jit(solution)/shard_map/ppermute | solution.py:101
  193.2 13.1 %collective-permute-start.33 = (bf16[2,1,1,1,1,96,384]{6,5,4,3,2,1,0:T(8,128)(2,1)S(1)}, bf16[2,1,1,1,1,96,384]{6,5,4,3,2,1,0:T(8,128)(2,1)S(1)}, u32[]{:S(2)}, u32[]{:S(2)}) collective-permute-start(bf16[2,1,1,1,1,96,384]{6,5,4,3,2,1,0:T(8,128)(2,1)S(1)} %constant_dynamic-slice_fusion.1), channel_id=1, source_target_pairs={{0,8},{1,9},{2,10},{3,11},{4,12},{5,13},{6,14},{7,15},{8,0},{9,1},... | collective-permute-start | bytes 442376 | tf_op jit(solution)/shard_map/ppermute | solution.py:101
  194.3 13.7 %collective-permute-start.28 = (bf16[2,1,1,1,1,96,384]{6,5,4,3,2,1,0:T(8,128)(2,1)S(1)}, bf16[2,1,1,1,1,96,384]{6,5,4,3,2,1,0:T(8,128)(2,1)S(1)}, u32[]{:S(2)}, u32[]{:S(2)}) collective-permute-start(bf16[2,1,1,1,1,96,384]{6,5,4,3,2,1,0:T(8,128)(2,1)S(1)} %constant_dynamic-slice_fusion.6), channel_id=1, source_target_pairs={{0,8},{1,9},{2,10},{3,11},{4,12},{5,13},{6,14},{7,15},{8,0},{9,1},... | collective-permute-start | bytes 442376 | tf_op jit(solution)/shard_map/ppermute | solution.py:101
  195.6 13.8 %collective-permute-start.14 = (bf16[1,1,1,1,1,24,1536]{6,5,4,3,2,1,0:T(8,128)(2,1)S(1)}, bf16[1,1,1,1,1,24,1536]{6,5,4,3,2,1,0:T(8,128)(2,1)S(1)}, u32[]{:S(2)}, u32[]{:S(2)}) collective-permute-start(bf16[1,1,1,1,1,24,1536]{6,5,4,3,2,1,0:T(8,128)(2,1)S(1)} %constant_dynamic-slice_fusion.20), channel_id=1, source_target_pairs={{0,16},{1,17},{2,18},{3,19},{4,20},{5,21},{6,22},{7,23},{8,24},{9,... | collective-permute-start | bytes 221192 | tf_op jit(solution)/shard_map/ppermute | solution.py:101
  197.8 13.4 %collective-permute-start.9 = (bf16[1,1,1,1,1,24,1536]{6,5,4,3,2,1,0:T(8,128)(2,1)S(1)}, bf16[1,1,1,1,1,24,1536]{6,5,4,3,2,1,0:T(8,128)(2,1)S(1)}, u32[]{:S(2)}, u32[]{:S(2)}) collective-permute-start(bf16[1,1,1,1,1,24,1536]{6,5,4,3,2,1,0:T(8,128)(2,1)S(1)} %constant_dynamic-slice_fusion.25), channel_id=1, source_target_pairs={{0,16},{1,17},{2,18},{3,19},{4,20},{5,21},{6,22},{7,23},{8,24},{9,... | collective-permute-start | bytes 221192 | tf_op jit(solution)/shard_map/ppermute | solution.py:101
  201.9 12.7 %collective-permute-start.24 = (bf16[1,1,1,1,1,24,1536]{6,5,4,3,2,1,0:T(8,128)(2,1)S(1)}, bf16[1,1,1,1,1,24,1536]{6,5,4,3,2,1,0:T(8,128)(2,1)S(1)}, u32[]{:S(2)}, u32[]{:S(2)}) collective-permute-start(bf16[1,1,1,1,1,24,1536]{6,5,4,3,2,1,0:T(8,128)(2,1)S(1)} %constant_dynamic-slice_fusion.10), channel_id=1, source_target_pairs={{0,16},{1,17},{2,18},{3,19},{4,20},{5,21},{6,22},{7,23},{8,24},{9,... | collective-permute-start | bytes 221192 | tf_op jit(solution)/shard_map/ppermute | solution.py:101
  206.3 10.7 %collective-permute-start.19 = (bf16[1,1,1,1,1,24,1536]{6,5,4,3,2,1,0:T(8,128)(2,1)S(1)}, bf16[1,1,1,1,1,24,1536]{6,5,4,3,2,1,0:T(8,128)(2,1)S(1)}, u32[]{:S(2)}, u32[]{:S(2)}) collective-permute-start(bf16[1,1,1,1,1,24,1536]{6,5,4,3,2,1,0:T(8,128)(2,1)S(1)} %constant_dynamic-slice_fusion.15), channel_id=1, source_target_pairs={{0,16},{1,17},{2,18},{3,19},{4,20},{5,21},{6,22},{7,23},{8,24},{9,... | collective-permute-start | bytes 221192 | tf_op jit(solution)/shard_map/ppermute | solution.py:101
  208.0 9.9 %collective-permute-start.34 = (bf16[1,1,1,1,1,96,384]{6,5,4,3,2,1,0:T(8,128)(2,1)S(1)}, bf16[1,1,1,1,1,96,384]{6,5,4,3,2,1,0:T(8,128)(2,1)S(1)}, u32[]{:S(2)}, u32[]{:S(2)}) collective-permute-start(bf16[1,1,1,1,1,96,384]{6,5,4,3,2,1,0:T(8,128)(2,1)S(1)} %constant_dynamic-slice_fusion), channel_id=1, source_target_pairs={{0,16},{1,17},{2,18},{3,19},{4,20},{5,21},{6,22},{7,23},{8,24},{9,... | collective-permute-start | bytes 221192 | tf_op jit(solution)/shard_map/ppermute | solution.py:101
  209.4 9.3 %collective-permute-start.29 = (bf16[1,1,1,1,1,96,384]{6,5,4,3,2,1,0:T(8,128)(2,1)S(1)}, bf16[1,1,1,1,1,96,384]{6,5,4,3,2,1,0:T(8,128)(2,1)S(1)}, u32[]{:S(2)}, u32[]{:S(2)}) collective-permute-start(bf16[1,1,1,1,1,96,384]{6,5,4,3,2,1,0:T(8,128)(2,1)S(1)} %constant_dynamic-slice_fusion.5), channel_id=1, source_target_pairs={{0,16},{1,17},{2,18},{3,19},{4,20},{5,21},{6,22},{7,23},{8,24},{9,... | collective-permute-start | bytes 221192 | tf_op jit(solution)/shard_map/ppermute | solution.py:101
  215.3 4.2 %copy-start.8 = (bf16[1,512,768]{2,1,0:T(8,128)(2,1)S(1)}, bf16[1,512,768]{2,1,0:T(8,128)(2,1)}, u32[]{:S(2)}) copy-start(bf16[1,512,768]{2,1,0:T(8,128)(2,1)} %get-tuple-element.66) | copy-start | bytes 2359300
  218.6 1.8 copy-start.7
where the time goes:
time: 222 us; the launch traced here: 221 us
  Pallas kernels  86.7 us (39%)
  waiting for transfers between devices  49.9 us (22%)
  starting transfers between devices  37.8 us (17%)
  local copies, waits for them, and re-layouts  30 us (14%)
  other arithmetic  15.5 us (7%)
    pallas_call x1, Pallas kernels, block_body(): pl.pallas_call(block_kernel, name='block', out_shape=(shape((1, rows, D),...  86.7 us
    ppermute x35, waiting for transfers between devices, scatter_stages(): came = lax.ppermute(sent, ('seq', 'blk'), swap)  49.9 us
    ppermute x35, starting transfers between devices, scatter_stages(): came = lax.ppermute(sent, ('seq', 'blk'), swap)  37.8 us
    dynamic_slice x35, local copies, waits for them, and re-layouts, scatter_stages(): sent = lax.dynamic_slice_in_dim(held, 1 - mine, 1, axis)  10.6 us
    slice x3, local copies, waits for them, and re-layouts, scatter_sum(): left = scatter_stages(terms[:, :, :width // 2], one)[0]  10.4 us
    convert_element_type x24, other arithmetic, scatter_stages(): held = total if number == bits - 1 else total.astype(kind)  9.58 us
  transfers between devices with their start and end apart: 35, of which 17 were waited for; matrix products, arithmetic and copies ran while one was open for 16% of the time, Pallas kernels for 0%

commit v1 on v0

--- a/solution.py
+++ b/solution.py
@@ -366,9 +366,23 @@
 bf16 = jnp.bfloat16
 MESH = pl.DeviceIdType.MESH
 PAIRS = HEADS // 2
-RING = 4
+RING = 3
 FF_CHUNK = 512
 ROW_TILE = 128
+ITEMS = 18
+ITEM_ROWS = 512
+ITEM_LANES = 768
+APART = 2
+SLOTS = 2 * APART
+STAGES = 5
+LANDING = (0, 256, 384, 448, 480)
+LANDING_ROWS = 496
+FLAT_BITS = ("y", "c", "x", "z0", "z1")
+GROUPS = (
+    (("c", "x", "y", "z0", "z1"), 0, 384),
+    (("c", "y", "x", "z0", "z1"), 384, 128),
+    (("c", "z0", "z1", "x", "y"), 512, 256),
+)
 
 
 def fits(mesh):
@@ -421,11 +435,19 @@
     fc2_bias,
     result_ref,
     gtok_ref,
-    vec_ref,
-    fb1_ref,
-    gfc1_hbm,
-    gfc2_hbm,
-    gqo_hbm,
+    out_ln1g,
+    out_ln1b,
+    out_qkv,
+    out_qb,
+    out_vb,
+    out_out,
+    out_ob,
+    out_ln2g,
+    out_ln2b,
+    out_fc1,
+    out_fb1,
+    out_fc2,
+    out_fb2,
     e_hbm,
     wqkv,
     wout,
@@ -443,21 +465,41 @@
     bias,
     ering,
     slots,
-    gfc1,
-    gfc2,
-    gn_out,
+    terms,
+    landing,
     gn_in,
     tags,
+    vec_ref,
+    fb1_ref,
+    small,
+    small_in,
     load_sem,
     e_sem,
-    out_sem,
     send_sem,
     recv_sem,
+    item_send,
+    item_recv,
+    small_send,
+    small_recv,
 ):
     rows = tok.shape[0]
     seq = lax.axis_index("seq")
     blk = lax.axis_index("blk")
-    twin = (seq, 1 - blk)
+    bit = {
+        "y": blk,
+        "c": lax.rem(seq, 2),
+        "x": lax.rem(seq // 2, 2),
+        "z0": lax.rem(seq // 4, 2),
+        "z1": seq // 8,
+    }
+    across = {
+        "y": (seq, 1 - blk),
+        "c": (seq + 1 - 2 * bit["c"], blk),
+        "x": (seq + 2 - 4 * bit["x"], blk),
+        "z0": (seq + 4 - 8 * bit["z0"], blk),
+        "z1": (seq + 8 - 16 * bit["z1"], blk),
+    }
+    twin = across["y"]
 
     loads = [
         pltpu.make_async_copy(src, dst, load_sem.at[i])
@@ -493,8 +535,9 @@
     tags[0] = jnp.where(padding == 1, -1, clips_at(lane_pos))
 
     barrier = pltpu.get_barrier_semaphore()
-    pl.semaphore_signal(barrier, inc=1, device_id=twin, device_id_type=MESH)
-    pl.semaphore_wait(barrier, 1)
+    for name in FLAT_BITS:
+        pl.semaphore_signal(barrier, inc=1, device_id=across[name], device_id_type=MESH)
+    pl.semaphore_wait(barrier, len(FLAT_BITS))
 
     def to_twin(i, src, dst):
         return pltpu.make_async_remote_copy(
@@ -510,6 +553,108 @@
     send_tags = to_twin(1, tags.at[0], tags.at[1])
     send_tags.start()
     send_tok.start()
+
+    def place_of(order, there):
+        at = 0
+        for stage, name in enumerate(order):
+            differs = there[name] + bit[name] - 2 * there[name] * bit[name]
+            at = at + (16 >> stage) * differs
+        return at
+
+    def bits_of(d):
+        return {name: (d >> i) & 1 for i, name in enumerate(FLAT_BITS)}
+
+    def item_copy(stage, item, group):
+        order, lane, width = GROUPS[group]
+        count = ITEM_ROWS >> stage
+        slot = lax.rem(item, SLOTS)
+        src_at = pl.multiple_of(item * ITEM_ROWS + count, 16)
+        dst_at = pl.multiple_of(slot * LANDING_ROWS + LANDING[stage - 1], 16)
+        sem = (slot * STAGES + stage - 1) * len(GROUPS) + group
+        return pltpu.make_async_remote_copy(
+            src_ref=terms.at[pl.ds(src_at, count), pl.ds(lane, width)],
+            dst_ref=landing.at[pl.ds(dst_at, count), pl.ds(lane, width)],
+            send_sem=item_send.at[sem],
+            recv_sem=item_recv.at[sem],
+            device_id=across[order[stage - 1]],
+            device_id_type=MESH,
+        )
+
+    def start_stage(stage, item):
+        for group in range(len(GROUPS)):
+            item_copy(stage, item, group).start()
+
+    def store_sum(item, kind, values):
+        if kind == 1:
+            at = pl.multiple_of((item - 6) * 16, 16)
+            out_fc2[pl.ds(at, 16), :] = values
+            return
+        parts = (
+            (0, 16, values[:, :256], values[:, 256:512]),
+            (16, 8, values[:8, 512:], values[8:, 512:]),
+        )
+        for top, count, left, right in parts:
+            here = pl.ds(top, count)
+            if kind == 0:
+                col = pl.multiple_of(item * 512, 512)
+                out_fc1[here, pl.ds(col, 256)] = left
+                out_fc1[here, pl.ds(col + 256, 256)] = right
+            else:
+                col = pl.multiple_of((item - 12) * 128, 128)
+                out_qkv[here, pl.ds(D + col, 128)] = left[:, :128]
+                out_qkv[here, pl.ds(2 * D + col, 128)] = left[:, 128:]
+                out_qkv[here, pl.ds(col, 128)] = right[:, :128]
+                out_out[here, pl.ds(col, 128)] = right[:, 128:]
+
+    def finish_stage(stage, item, low, high):
+        for group in range(len(GROUPS)):
+            item_copy(stage, item, group).wait()
+        count = ITEM_ROWS >> stage
+        slot = lax.rem(item, SLOTS)
+        here = pl.ds(pl.multiple_of(item * ITEM_ROWS, 16), count)
+        came = pl.ds(pl.multiple_of(slot * LANDING_ROWS + LANDING[stage - 1], 16), count)
+        if stage < STAGES:
+            terms[here, :] = terms[here, :] + landing[came, :]
+            start_stage(stage + 1, item)
+            return
+        values = terms[here, :].astype(f32) + landing[came, :].astype(f32)
+        for kind in range(3):
+            if high < 6 * kind or low >= 6 * kind + 6:
+                continue
+            if low >= 6 * kind and high < 6 * kind + 6:
+                store_sum(item, kind, values)
+            else:
+                pl.when((item >= 6 * kind) & (item < 6 * kind + 6))(
+                    functools.partial(store_sum, item, kind, values)
+                )
+
+    def tick(number, low, high):
+        number = jnp.int32(number)
+        for stage in range(STAGES, 0, -1):
+            first, last = low - APART * stage, high - APART * stage
+            if last < 0 or first >= ITEMS:
+                continue
+            item = number - APART * stage
+            act = functools.partial(
+                finish_stage, stage, item, max(first, 0), min(last, ITEMS - 1)
+            )
+            if first >= 0 and last < ITEMS:
+                act()
+            else:
+                pl.when((item >= 0) & (item < ITEMS))(act)
+        if high < ITEMS:
+            start_stage(1, number)
+
+    def put_24(item, values):
+        base_row = item * ITEM_ROWS
+        for d in range(32):
+            top = values[24 * d : 24 * d + 16, :]
+            rest = values[24 * d + 16 : 24 * d + 24, :]
+            rest = jnp.concatenate([rest[:, :256], rest[:, 256:]], axis=0)
+            block = jnp.concatenate([top, rest], axis=1).astype(bf16)
+            for order, lane, width in GROUPS:
+                at = pl.multiple_of(base_row + 16 * place_of(order, bits_of(d)), 16)
+                terms[pl.ds(at, 16), lane : lane + width] = block[:, lane : lane + width]
 
     row_tiles = rows // ROW_TILE
 
@@ -672,19 +817,40 @@
         grad_pre = (dot_nt(cot[...], w2) * slope).astype(bf16)
         slots[ACC] += dot(activated, w2)
         slots[GNT] += dot_nt(grad_pre, w1)
-        gfc2[units, :] = dot_tn(activated, cot[...]).astype(bf16)
-        gfc1[:, units] = dot(nrm2_t[...], grad_pre).astype(bf16)
-        fb1_ref[:, units] = column_sum(grad_pre.astype(f32))
+        ering[c // 2, lax.rem(c, 2)] = activated
+        fb1_ref[0:1, units] = column_sum(grad_pre.astype(f32))
+        put_24(c, dot(nrm2_t[...], grad_pre))
+        tick(c, 0, FF // FF_CHUNK - 1)
         return carry
-
-    lax.fori_loop(0, FF // FF_CHUNK, feed, 0)
-    store_fc1 = pltpu.make_async_copy(gfc1, gfc1_hbm, out_sem.at[0])
-    store_fc2 = pltpu.make_async_copy(gfc2, gfc2_hbm, out_sem.at[1])
-    store_fc1.start()
-    store_fc2.start()
 
     for number in range(2 * PAIRS - RING, 2 * PAIRS):
         e_copy(number, number % RING, True).wait()
+    lax.fori_loop(0, FF // FF_CHUNK, feed, 0)
+
+    def weight_fc2(c, carry):
+        pieces = []
+        for p in range(3):
+            piece = 3 * c + p
+            chunk = piece // 2
+            lanes = pl.ds(pl.multiple_of(256 * lax.rem(piece, 2), 256), 256)
+            part = ering[chunk // 2, lax.rem(chunk, 2), :, lanes]
+            pieces.append(dot_tn(part, cot[...]))
+        values = jnp.concatenate(pieces, axis=0)
+        for low in range(8):
+            there = bits_of(low)
+            there["z0"] = lax.rem(c, 2)
+            there["z1"] = c // 2
+            for order, lane, width in GROUPS:
+                place = 16 * place_of(order, there)
+                for j in range(6):
+                    top = 96 * low + 16 * j
+                    block = values[top : top + 16, lane : lane + width].astype(bf16)
+                    at = pl.multiple_of((6 + j) * ITEM_ROWS + place, 16)
+                    terms[pl.ds(at, 16), lane : lane + width] = block
+        return carry
+
+    lax.fori_loop(0, 4, weight_fc2, 0)
+    tick(6, 6, 6)
     back_order = [PAIRS + hp for hp in range(PAIRS)] + list(range(PAIRS))
 
     def e_number(step):
@@ -694,6 +860,7 @@
         e_copy(back_order[step], step % RING, False).start()
 
     vec_ref[...] = jnp.zeros(vec_ref.shape, f32)
+    fb1_ref[1:8, :] = jnp.zeros((7, FF), f32)
     (V_LN1G, V_LN1B, V_QB, V_VB, V_OB, V_LN2G, V_LN2B, V_FC2B) = range(8)
 
     def add_vec(kind, values):
@@ -723,6 +890,7 @@
         return carry
 
     lax.fori_loop(0, row_tiles, second_back, 0)
+    tick(7, 7, 7)
 
     GQ = ACC
 
@@ -730,10 +898,11 @@
         cols = pl.ds(pl.multiple_of(c * wide, wide), wide)
         gm[:, cols] = dot_nt(nrm[...], wout[cols, :]).astype(bf16)
         mixed = slots[MIXED, :, cols].astype(bf16)
-        wfc1[cols, 3 * D : 4 * D] = dot_tn(mixed, nrm[...]).astype(bf16)
+        wfc1[cols, :D] = dot_tn(mixed, nrm[...]).astype(bf16)
         return carry
 
     lax.fori_loop(0, D // wide, mixed_back, 0)
+    tick(8, 8, 8)
 
     def backward_pair(part, hp, key_ref, key_at, value_at):
         col = pl.multiple_of(hp * 128, 128)
@@ -774,50 +943,45 @@
             total_q = (slots[GQ, :, cols] + grad_q) * score_scale
             qkv[:, cols] = total_q.astype(bf16)
 
-    pairs_loop(lambda hp: backward_pair(1, hp, kvp, 0, D))
+    def twin_step(step, carry):
+        for p in range(2):
+            backward_pair(1, 2 * step + p, kvp, 0, D)
+        tick(9 + step, 9, 11)
+        return carry
+
+    lax.fori_loop(0, PAIRS // 2, twin_step, 0)
 
     def partial_out(c, carry):
         cols = pl.ds(pl.multiple_of(c * wide, wide), wide)
-        gn_out[:, cols] = dot_nt(kvp[...], wqkv[cols, D : 3 * D]).astype(bf16)
+        tokp[:, cols] = dot_nt(kvp[...], wqkv[cols, D : 3 * D]).astype(bf16)
         return carry
 
     lax.fori_loop(0, D // wide, partial_out, 0)
-    send_gn = to_twin(2, gn_out, gn_in)
+    send_gn = to_twin(2, tokp, gn_in)
     send_gn.start()
 
-    pairs_loop(lambda hp: backward_pair(0, hp, qkv, D, 2 * D))
-
-    def weight_own(c, carry):
-        cols = pl.ds(pl.multiple_of(c * wide, wide), wide)
-        wfc1[:, cols] = dot(nrm_t[:, :rows], qkv[:, cols]).astype(bf16)
-        add_vec_cols(V_QB, cols, qkv[:, cols])
+    def own_step(hp, carry):
+        backward_pair(0, hp, qkv, D, 2 * D)
+        col = pl.multiple_of(hp * 128, 128)
+        grad_q = qkv[:, pl.ds(col, 128)]
+        own = jnp.concatenate(
+            [qkv[:, pl.ds(D + col, 128)], qkv[:, pl.ds(2 * D + col, 128)]], axis=1
+        )
+        other = jnp.concatenate(
+            [kvp[:, pl.ds(col, 128)], kvp[:, pl.ds(D + col, 128)]], axis=1
+        )
+        vec_ref[V_QB : V_QB + 1, pl.ds(col, 128)] = column_sum(grad_q.astype(f32))
+        vec_ref[V_VB : V_VB + 1, pl.ds(col, 128)] = column_sum(
+            own[:, 128:].astype(f32) + other[:, 128:].astype(f32)
+        )
+        weight_kv = dot(nrm_t[...], jnp.concatenate([own, other], axis=0))
+        weight_q = dot(nrm_t[:, :rows], grad_q)
+        weight_o = wfc1[:, pl.ds(col, 128)].astype(f32)
+        put_24(12 + hp, jnp.concatenate([weight_kv, weight_q, weight_o], axis=1))
+        tick(12 + hp, 12, 17)
         return carry
 
-    def add_vec_cols(kind, cols, values):
-        vec_ref[kind : kind + 1, cols] = column_sum(values.astype(f32))
-
-    lax.fori_loop(0, D // wide, weight_own, 0)
-
-    def weight_both(c, carry):
-        col = pl.multiple_of(c * wide, wide)
-        own = qkv[:, pl.ds(D + col, wide)]
-        other = kvp[:, pl.ds(col, wide)]
-        joint = jnp.concatenate([own, other], axis=0)
-        wfc1[:, pl.ds(D + col, wide)] = dot(nrm_t[...], joint).astype(bf16)
-        return carry
-
-    lax.fori_loop(0, 2 * D // wide, weight_both, 0)
-    store_qo = pltpu.make_async_copy(wfc1, gqo_hbm, out_sem.at[2])
-    store_qo.start()
-
-    def value_sum(c, carry):
-        col = pl.multiple_of(c * wide, wide)
-        values = qkv[:, pl.ds(2 * D + col, wide)].astype(f32)
-        other = kvp[:, pl.ds(D + col, wide)].astype(f32)
-        vec_ref[V_VB : V_VB + 1, pl.ds(col, wide)] = column_sum(values + other)
-        return carry
-
-    lax.fori_loop(0, D // wide, value_sum, 0)
+    lax.fori_loop(0, PAIRS, own_step, 0)
 
     def first_back_product(c, carry):
         cols = pl.ds(pl.multiple_of(c * wide, wide), wide)
@@ -825,6 +989,7 @@
         return carry
 
     lax.fori_loop(0, D // wide, first_back_product, 0)
+    tick(18, 18, 18)
     send_gn.wait()
     gain_one = row(ln1_gain)
 
@@ -844,9 +1009,51 @@
         return carry
 
     lax.fori_loop(0, row_tiles, first_back, 0)
-    store_fc1.wait()
-    store_fc2.wait()
-    store_qo.wait()
+    tick(19, 19, 19)
+
+    def window(ref, first, count):
+        block = first // 128 * 128
+        shift = first - block
+        wide_enough = 256 if shift + count > 128 else 128
+        piece = ref[:, block : block + wide_enough]
+        if shift:
+            piece = pltpu.roll(piece, wide_enough - shift, 1)
+        return piece[:, :128]
+
+    small_order = GROUPS[0][0]
+    for d in range(32):
+        at = pl.multiple_of(16 * place_of(small_order, bits_of(d)), 16)
+        small[pl.ds(at, 8), :] = window(vec_ref, 24 * d, 24)
+        small[pl.ds(at + 8, 8), :] = window(fb1_ref, 96 * d, 96)
+
+    def small_copy(stage):
+        count = ITEM_ROWS >> stage
+        return pltpu.make_async_remote_copy(
+            src_ref=small.at[pl.ds(count, count)],
+            dst_ref=small_in.at[pl.ds(LANDING[stage - 1], count)],
+            send_sem=small_send.at[stage - 1],
+            recv_sem=small_recv.at[stage - 1],
+            device_id=across[small_order[stage - 1]],
+            device_id_type=MESH,
+        )
+
+    small_copy(1).start()
+    for number in range(20, ITEMS + APART * STAGES):
+        tick(number, number, number)
+        if number % 2 == 1:
+            stage = (number - 19) // 2
+            count = ITEM_ROWS >> stage
+            small_copy(stage).wait()
+            small[:count] = small[:count] + small_in[LANDING[stage - 1] : LANDING[stage - 1] + count]
+            if stage < STAGES:
+                small_copy(stage + 1).start()
+    small_copy(STAGES).wait()
+    summed = small[:16] + small_in[LANDING[4] : LANDING[4] + 16]
+    for kind, ref in enumerate(
+        (out_ln1g, out_ln1b, out_qb, out_vb, out_ob, out_ln2g, out_ln2b, out_fb2)
+    ):
+        ref[...] = summed[kind, :24]
+    out_fb1[...] = summed[8, :96]
 
 
 def block_body(
@@ -874,24 +1081,34 @@
     any_spec = pl.BlockSpec(memory_space=pl.ANY)
     vmem = pl.BlockSpec(memory_space=pltpu.VMEM)
     smem = pl.BlockSpec(memory_space=pltpu.SMEM)
-    result, grad_tokens, vec, fb1, gfc1, gfc2, gqo, _ = pl.pallas_call(
+    part = D // n_dev
+    line = shape((part,), f32)
+    outs = pl.pallas_call(
         block_kernel,
         name="block",
         out_shape=(
             shape((1, rows, D), bf16),
             shape((1, rows, D), bf16),
-            shape((8, D), f32),
-            shape((1, FF), f32),
-            shape((D, FF), bf16),
-            shape((FF, D), bf16),
-            shape((D, 4 * D), bf16),
+            line,
+            line,
+            shape((part, 3 * D), f32),
+            line,
+            line,
+            shape((part, D), f32),
+            line,
+            line,
+            line,
+            shape((part, FF), f32),
+            shape((FF // n_dev,), f32),
+            shape((FF // n_dev, D), f32),
+            line,
             shape((2 * PAIRS, 2, rows, rows), bf16),
         ),
         in_specs=[
             any_spec, smem, vmem, any_spec, vmem, vmem, any_spec, vmem, vmem,
             any_spec, vmem, vmem, vmem, any_spec, vmem, any_spec, vmem,
         ],
-        out_specs=(vmem, vmem, vmem, vmem, any_spec, any_spec, any_spec, any_spec),
+        out_specs=(vmem,) * 15 + (any_spec,),
         scratch_shapes=[
             pltpu.VMEM((D, 3 * D), bf16),
             pltpu.VMEM((D, D), bf16),
@@ -909,16 +1126,22 @@
             pltpu.VMEM((rows, rows), f32),
             pltpu.VMEM((RING, 2, rows, rows), bf16),
             pltpu.VMEM((6, rows, D), f32),
-            pltpu.VMEM((D, FF), bf16),
-            pltpu.VMEM((FF, D), bf16),
-            pltpu.VMEM((rows, D), bf16),
+            pltpu.VMEM((ITEMS * ITEM_ROWS, ITEM_LANES), bf16),
+            pltpu.VMEM((SLOTS * LANDING_ROWS, ITEM_LANES), bf16),
             pltpu.VMEM((rows, D), bf16),
             pltpu.VMEM((2, 8, rows), jnp.int32),
+            pltpu.VMEM((8, D), f32),
+            pltpu.VMEM((8, FF), f32),
+            pltpu.VMEM((ITEM_ROWS, 128), f32),
+            pltpu.VMEM((LANDING_ROWS, 128), f32),
             pltpu.SemaphoreType.DMA((6,)),
             pltpu.SemaphoreType.DMA((RING,)),
             pltpu.SemaphoreType.DMA((3,)),
             pltpu.SemaphoreType.DMA((3,)),
-            pltpu.SemaphoreType.DMA((3,)),
+            pltpu.SemaphoreType.DMA((SLOTS * STAGES * len(GROUPS),)),
+            pltpu.SemaphoreType.DMA((SLOTS * STAGES * len(GROUPS),)),
+            pltpu.SemaphoreType.DMA((STAGES,)),
+            pltpu.SemaphoreType.DMA((STAGES,)),
         ],
         compiler_params=pltpu.CompilerParams(
             collective_id=0, has_side_effects=True, vmem_limit_bytes=VMEM_LIMIT
@@ -930,35 +1153,10 @@
         tokens, lengths, padding, cotangent, ln1_gain, ln1_bias, w_qkv, q_bias, v_bias,
         w_out, out_bias, ln2_gain, ln2_bias, w_fc1, fc1_bias, w_fc2, fc2_bias,
     )
-    small = jnp.concatenate(
-        [vec[k].reshape(n_dev, -1) for k in range(8)] + [fb1.reshape(n_dev, -1)], axis=1
-    )
-    sum_fc2 = scatter_sum(gfc2)
-    sum_fc1 = scatter_sum(gfc1)
-    sum_qo = scatter_sum(gqo)
-    small = scatter_stages(small, stage_orders()[0])[0]
-    part = D // n_dev
-    one = [small[k * part : (k + 1) * part] for k in range(8)]
-    return (
-        result,
-        grad_tokens,
-        one[0],
-        one[1],
-        sum_qo[:, : 3 * D],
-        one[2],
-        one[3],
-        sum_qo[:, 3 * D :],
-        one[4],
-        one[5],
-        one[6],
-        sum_fc1,
-        small[8 * part :],
-        sum_fc2,
-        one[7],
-    )
-
-
-VMEM_LIMIT = 62 * 2**20
+    return outs[:15]
+
+
+VMEM_LIMIT = 63 * 2**20
 
 
 def solution(mesh):

time: 222 us -> 152 us (0.68)
  waiting for transfers between devices: 49.9 us -> 0 us
  Pallas kernels: 86.7 us -> 130 us
  starting transfers between devices: 37.8 us -> 0 us
  other arithmetic: 15.5 us -> 0 us
  local copies, waits for them, and re-layouts: 30 us -> 20.5 us
    ppermute x35 -> x0, waiting for transfers between devices: 49.9 us -> none  [scatter_stages(): came = lax.ppermute(sent, ('seq', 'blk'), swap)]
    pallas_call x1, Pallas kernels: 86.7 us -> 130 us  [block_body(): pl.pallas_call(block_kernel, name='block', out_shape=(shape((1, rows, D),...]
    ppermute x35 -> x0, starting transfers between devices: 37.8 us -> none  [scatter_stages(): came = lax.ppermute(sent, ('seq', 'blk'), swap)]
    unnamed x28 -> x17, local copies, waits for them, and re-layouts: 4.32 us -> 20.5 us
    slice x7 -> x0, local copies, waits for them, and re-layouts: 13.5 us -> none  [the longest x3 10.4 us: scatter_sum(): left = scatter_stages(terms[:, :, :width // 2], one)[0]]
    dynamic_slice x35 -> x0, local copies, waits for them, and re-layouts: 10.6 us -> none  [scatter_stages(): sent = lax.dynamic_slice_in_dim(held, 1 - mine, 1, axis)]
    convert_element_type x24 -> x0, other arithmetic: 9.58 us -> none  [scatter_stages(): held = total if number == bits - 1 else total.astype(kind)]
  transfers between devices with their start and end apart: 35 -> 0, of which waited for: 17 -> 0; matrix products, arithmetic and copies ran while one was open for 16% -> 0% of each run, Pallas kernels for 0% -> 0%
where the time goes in v1:
time: 152 us
  Pallas kernels  130 us (86%)
  local copies, waits for them, and re-layouts  20.5 us (13%)
    pallas_call x1, Pallas kernels, block_body(): pl.pallas_call(block_kernel, name='block', out_shape=(shape((1, rows, D),...  130 us
    unnamed x17, local copies, waits for them, and re-layouts  20.5 us

profile of v1, /device:TPU:0, one launch (start us, length us, event | category | flops | bytes accessed | tf_op | source)
XLA Modules:
  0.0 151.6 jit_solution(10249453834021058242)
XLA Ops:
  0.7 130.5 %block.1 = (bf16[1,512,768]{2,1,0:T(8,128)(2,1)}, bf16[1,512,768]{2,1,0:T(8,128)(2,1)}, f32[24]{0:T(128)}, f32[24]{0:T(128)}, f32[24,2304]{1,0:T(8,128)}, /*inde...) custom-call(bf16[1,512,768]{2,1,0:T(8,128)(2,1)} %tok_hbm.1, ...), custom_call_target="tpu_custom_call" | custom-call | flops 30000001024 | bytes 60000000 | tf_op jit(solution)/shard_map/block/pallas_call | solution.py:1086
  131.1 0.0 copy-start
  131.1 2.1 %copy.47 = bf16[1,512,768]{2,1,0:T(8,128)(2,1)} copy(bf16[1,512,768]{2,1,0:T(8,128)(2,1)} %get-tuple-element.60) | data formatting | bytes 1572864
  133.2 2.1 %copy.48 = bf16[1,512,768]{2,1,0:T(8,128)(2,1)} copy(bf16[1,512,768]{2,1,0:T(8,128)(2,1)} %get-tuple-element.61) | data formatting | bytes 1572864
  135.2 1.2 copy.49
  136.4 1.1 copy.50
  137.5 1.6 %copy.51 = f32[24,2304]{1,0:T(8,128)} copy(f32[24,2304]{1,0:T(8,128)} %get-tuple-element.64) | data formatting | bytes 442368
  139.2 1.1 copy.52
  140.3 1.2 copy.53
  141.5 1.5 %copy.54 = f32[24,768]{1,0:T(8,128)} copy(f32[24,768]{1,0:T(8,128)} %get-tuple-element.67) | data formatting | bytes 147456
  143.0 1.2 copy.55
  144.2 1.2 copy.56
  145.4 1.1 copy.57
  146.5 1.7 %copy.58 = f32[24,3072]{1,0:T(8,128)} copy(f32[24,3072]{1,0:T(8,128)} %get-tuple-element.71) | data formatting | bytes 589824
  148.2 1.2 copy.59
  149.4 1.7 %copy.60 = f32[96,768]{1,0:T(8,128)} copy(f32[96,768]{1,0:T(8,128)} %get-tuple-element.73) | data formatting | bytes 589824
  151.1 0.0 copy-done
  151.1 0.5 copy.61
Async XLA Ops:
  131.1 20.0 %copy-start = (f32[24]{0:T(128)S(1)}, f32[24]{0:T(128)}, u32[]{:S(2)}) copy-start(f32[24]{0:T(128)} %get-tuple-element.74) | copy-start | bytes 292
